TPU v7x, 256 devices: a whole 4x4x8 slice. The times are simulated.
256 devices in a mesh: dp: 128 (over y_lo, x, z, core), tensor: 2 (over y_hi).
Axes of the slice: x: 4, y: 4 (y_hi: 2, y_lo: 2; y = y_hi * 2 + y_lo), z: 8, core: 2. Of those that a mesh axis runs over, the one named last changes fastest.
Arguments:
- images: bfloat16 [32768, 2048], P('dp'), may hold values from -24 to 24
- texts: bfloat16 [32768, 4096], P('dp', 'tensor'), may hold values from -6 to 6
- head: bfloat16 [2048, 4096], P(None, 'tensor'), may hold values from -0.125 to 0.125
- pair_mask: int32 [128, 4], P('dp'), may hold values 0 or 1
- labels: int32 [32768], P('dp'), may hold values from 0 to 1023
- logit_scale: float32 [1], replicated, may hold values from 8 to 16
- logit_bias: float32 [1], replicated, may hold values from -3 to -1
Outputs:
- grad_images: bfloat16 [32768, 2048], P('dp', 'tensor')
- grad_texts: bfloat16 [32768, 4096], P('dp', 'tensor')
- grad_head: float32 [2048, 4096], P('dp', 'tensor')
All inputs are finite; a program needn't handle non-finite values. No bound on the sum of `pair_mask` on one device may be relied on, other than what follows from the above.
Results may differ from a plain program's by a relative error of at most 0.0063.
Values may be sent and summed in bfloat16 or wider, within the bound.
No kernel may reach another device: no remote copies, remote signals or barrier semaphores. Data moves between devices by JAX's collectives and lax.ppermute only.
A program may use at most 128 MiB of HBM per device.

v0:
```python
import jax
import jax.numpy as jnp
from jax import lax
from jax.experimental import pallas as pl
from jax.experimental.pallas import tpu as pltpu
from jax.sharding import PartitionSpec as P

EPSILON = 1e-06
LOSS_WEIGHT = 16.0
YS, XS, ZS, CORES = 2, 4, 8, 2

F32 = jnp.float32
BF16 = jnp.bfloat16


def place(index):
    return index // (XS * ZS * CORES), index // (ZS * CORES) % XS, index // CORES % ZS, index % CORES


def index_of(y, x, z, core):
    return (((y % YS) * XS + x % XS) * ZS + z % ZS) * CORES + core % CORES


def route(target):
    return [(i, target(i) % (YS * XS * ZS * CORES)) for i in range(YS * XS * ZS * CORES)]


def send(block, target):
    return lax.ppermute(block, "dp", route(target))


def swap_tensor(block):
    return lax.ppermute(block, "tensor", [(0, 1), (1, 0)])


def over_x(distance):
    def target(i):
        y, x, z, core = place(i)
        return index_of(y, x + distance, z, core)

    return target


def over_z(distance):
    def target(i):
        y, x, z, core = place(i)
        return index_of(y, x, z + distance, core)

    return target


def over_y(i):
    y, x, z, core = place(i)
    return index_of(y + 1, x, z, core)


def other_core(i):
    return i ^ 1


def dot(a, b, left, right):
    return lax.dot_general(a, b, (((left,), (right,)), ((), ())), preferred_element_type=F32)


EXTRA = 16


def nothing(*refs):
    pass


def gate(value, *earlier):
    spec = pl.BlockSpec(memory_space=pl.ANY)
    return pl.pallas_call(
        nothing,
        out_shape=jax.ShapeDtypeStruct(value.shape, value.dtype),
        in_specs=[spec] * (1 + len(earlier)),
        out_specs=spec,
        input_output_aliases={0: 0},
        compiler_params=pltpu.CompilerParams(vmem_limit_bytes=48 * 1024 * 1024),
    )(value, *earlier)


def call(kernel, outs, ins, operands, grid=None, scratch=(), vmem=48, cost=0):
    shapes = [jax.ShapeDtypeStruct(shape, dtype) for shape, dtype, _ in outs]
    return pl.pallas_call(
        kernel,
        out_shape=shapes,
        grid=grid or (1,),
        in_specs=ins,
        out_specs=[spec for _, _, spec in outs],
        scratch_shapes=list(scratch),
        compiler_params=pltpu.CompilerParams(vmem_limit_bytes=vmem * 1024 * 1024),
        cost_estimate=pl.CostEstimate(flops=cost, bytes_accessed=cost // 512, transcendentals=0),
    )(*operands)


def whole(shape):
    return pl.BlockSpec(shape, lambda j: (0,) * len(shape))


def strip(rows, columns):
    return pl.BlockSpec((rows, columns), lambda j: (0, j))


SCALAR = pl.BlockSpec(memory_space=pltpu.SMEM)
LATER = pl.BlockSpec(memory_space=pl.ANY)


def diagonal(n):
    return lax.broadcasted_iota(jnp.int32, (n, n), 0) == lax.broadcasted_iota(jnp.int32, (n, n), 1)


def to_row(column):
    return jnp.sum(jnp.where(diagonal(column.shape[0]), column, 0.0), axis=0, keepdims=True)


def to_column(row):
    return jnp.sum(jnp.where(diagonal(row.shape[1]), row, 0.0), axis=1, keepdims=True)


def message(part, *rows):
    n = part.shape[1]
    line = lax.broadcasted_iota(jnp.int32, (EXTRA, n), 0)
    extra = jnp.zeros((EXTRA, n), F32)
    for k, row in enumerate(rows):
        high = row.astype(BF16).astype(F32)
        extra = jnp.where(line == 2 * k, high, jnp.where(line == 2 * k + 1, row - high, extra))
    return jnp.concatenate([part.astype(BF16), extra.astype(BF16)], axis=0)


def row_of(extra, k):
    extra = extra.astype(F32)
    return extra[2 * k : 2 * k + 1] + extra[2 * k + 1 : 2 * k + 2]


def square_sum(block):
    block = block.astype(F32)
    return jnp.sum(block * block, axis=1, keepdims=True)


def project_kernel(images, head, texts, projected, projected_b, part, sent, squares, own):
    step = pl.program_id(0)
    product = jnp.dot(images[...], head[...], preferred_element_type=F32)
    projected[...] = product
    rounded = product.astype(BF16)
    projected_b[...] = rounded
    score = dot(rounded, texts[...], 1, 1)
    square_text = square_sum(texts[...])
    square_image = square_sum(product)

    @pl.when(step == 0)
    def _():
        part[...] = score
        own[:, 0:1] = square_text
        own[:, 1:2] = square_image

    @pl.when(step > 0)
    def _():
        part[...] += score
        own[:, 0:1] += square_text
        own[:, 1:2] += square_image

    @pl.when(step == pl.num_programs(0) - 1)
    def _():
        text_row, image_row = to_row(own[:, 0:1]), to_row(own[:, 1:2])
        line = lax.broadcasted_iota(jnp.int32, squares.shape, 0)
        squares[...] = jnp.where(line == 0, text_row, image_row)
        sent[...] = message(part[...], text_row, image_row)


def tile_kernel(rounded, text, part, sent, squares):
    part[...] = dot(rounded[...], text[...], 1, 1)
    row = to_row(square_sum(text[...]))
    squares[...] = jnp.broadcast_to(row, squares.shape)
    sent[...] = message(part[...], row)


def near_kernel(rounded, text, before, part, sent, squares):
    part[...] = dot(rounded[...], text[...], 1, 1)
    row = to_row(square_sum(text[...]))
    squares[...] = jnp.broadcast_to(row, squares.shape)
    sent[0] = before[...]
    sent[1] = message(part[...], row)


def far_kernel(core, rounded, first, second, far, part, sent, squares):
    @pl.when(core[0] == 0)
    def _():
        far[...] = first[...]

    @pl.when(core[0] != 0)
    def _():
        far[...] = second[...]

    part[...] = dot(rounded[...], far[...], 1, 1)
    row = to_row(square_sum(far[...]))
    squares[...] = jnp.broadcast_to(row, squares.shape)
    sent[...] = message(part[...], row)


def coefficients(part, there, square_row, inverse_image, labels, offset, mask, scale, bias):
    n = part.shape[0]
    inverse = lax.rsqrt(square_row + row_of(there[n:], 0) + EPSILON)
    scores = (part + there[:n].astype(F32)) * inverse_image * inverse
    logits = scale * scores + bias
    columns = lax.broadcasted_iota(jnp.int32, (n, n), 1) + offset * n
    sign = jnp.where(labels == columns, 1.0, -1.0)
    weight = mask.astype(F32)
    result = (-LOSS_WEIGHT * scale * weight) * sign * jax.nn.sigmoid(-sign * logits)
    inner = jnp.sum(result * scores, axis=1, keepdims=True)
    back = result * inverse_image
    return (result * inverse).astype(BF16), inner, back, inverse


def some_kernel(
    core, scale, bias, mask, labels, own_part, own_squares, near_part, near_there, near_squares,
    cross_part, cross_there, cross_squares, texts, near, cross, later,
    pull, own_back, near_back, cross_back, inner, inverses, weights,
):
    @pl.when(pl.program_id(0) == 0)
    def _():
        n = own_part.shape[0]
        image_row = own_squares[1:2, :] + row_of(near_there[0][n:], 1)
        inverse_image = to_column(lax.rsqrt(image_row + EPSILON))
        label = to_column(labels[...].astype(F32)).astype(jnp.int32)
        rest = (inverse_image, label)
        total = jnp.zeros((n, 1), F32)
        which = 1 + 2 * core[0]
        tiles = (
            (own_part[...], near_there[0], own_squares[0:1, :], 0, own_back),
            (near_part[...], near_there[1], near_squares[0:1, :], 2, near_back),
            (cross_part[...], cross_there[...], cross_squares[0:1, :], which, cross_back),
        )
        for k, (part, there, row, offset, out) in enumerate(tiles):
            weight, dots, back, inverse = coefficients(
                part, there, row, *rest, offset, mask[0, offset], scale[0], bias[0]
            )
            weights[k] = weight
            out[...] = back.T.astype(BF16)
            total = total + dots
            if k == 0:
                inverses[:, 1:2] = to_column(inverse)
        inner[...] = total
        inverses[:, 0:1] = inverse_image

    pull[...] = (
        dot(weights[0], texts[...], 1, 0)
        + dot(weights[1], near[...], 1, 0)
        + dot(weights[2], cross[...], 1, 0)
    )


def unit_kernel(
    core, scale, bias, mask, labels, part, there, squares, far, pull, inner, inverses, projected,
    later_a, later_b, unit, back, weight, factor,
):
    @pl.when(pl.program_id(0) == 0)
    def _():
        inverse_image = inverses[:, 0:1]
        label = to_column(labels[...].astype(F32)).astype(jnp.int32)
        offset = 3 - 2 * core[0]
        weights, dots, backs, _ = coefficients(
            part[...], there[...], squares[0:1, :], inverse_image, label, offset,
            mask[0, offset], scale[0], bias[0],
        )
        weight[...] = weights
        back[...] = backs.astype(BF16)
        factor[...] = inverse_image * (inner[...] + dots)

    total = pull[...] + dot(weight[...], far[...], 1, 0)
    unit[...] = ((total - projected[...] * factor[...]) * inverses[:, 0:1]).astype(BF16)


def turned_kernel(place_ref, images, mine, theirs, turned):
    turned[...] = images[...].astype(F32).T.astype(BF16)
    unit = mine.shape[0] // (YS * XS * ZS)
    core, here_x, here_y = place_ref[0], place_ref[1], place_ref[2]
    for dy in range(YS):
        for dx in range(XS):
            x, y = (here_x + dx) & (XS - 1), (here_y + dy) & (YS - 1)
            for z in range(ZS):
                to = ((dy * XS + dx) * ZS + z) * unit
                block = ((y * XS + x) * ZS + z) * CORES
                for whose, out in ((core, mine), (1 - core, theirs)):
                    start = pl.multiple_of((block + whose) * unit, unit)
                    out[to : to + unit, :] = turned[pl.ds(start, unit), :]


def send_kernel(mine, theirs, own, pair, a1, a2, a3, send_b, left, right):
    slab = mine.shape[0] // (YS * XS)
    many = (XS - 1) * slab

    @pl.when(pl.program_id(0) == 0)
    def _():
        for dy in range(YS):
            rows = slice((dy * XS + 1) * slab, (dy * XS + XS) * slab)
            left[dy * many : (dy + 1) * many, :] = mine[rows, :]
            right[dy * many : (dy + 1) * many, :] = theirs[rows, :]

    @pl.when(pl.program_id(0) < pl.num_programs(0) // 2)
    def _():
        total = dot(left[...], own[...], 1, 0) + dot(right[...], pair[...], 1, 0)
        total = total.astype(BF16)
        for dy in range(YS):
            for k, out in enumerate((a1, a2, a3)):
                start = dy * many + k * slab
                out[dy * slab : (dy + 1) * slab, :] = total[start : start + slab]

    @pl.when(pl.program_id(0) >= pl.num_programs(0) // 2)
    def _():
        rows = slice(XS * slab, 2 * XS * slab)
        total = dot(mine[rows, :], own[...], 1, 0) + dot(theirs[rows, :], pair[...], 1, 0)
        send_b[...] = total.astype(BF16)


def sum_a_kernel(mine, theirs, own, pair, g1, g2, g3, keep, sent):
    slab = mine.shape[0] // (YS * XS)
    for dy in range(YS):
        rows = slice(dy * XS * slab, (dy * XS + 1) * slab)
        total = dot(mine[rows, :], own[...], 1, 0) + dot(theirs[rows, :], pair[...], 1, 0)
        for got in (g1, g2, g3):
            total = total + got[dy * slab : (dy + 1) * slab, :].astype(F32)
        if dy == 0:
            keep[...] = total
        else:
            sent[...] = total.astype(BF16)


def sum_b_kernel(mine, theirs, own, pair, got, later, keep, s1, s2, s3):
    slab = mine.shape[0] // (YS * XS)
    rows = slice(0, XS * slab)
    total = dot(mine[rows, :], own[...], 1, 0) + dot(theirs[rows, :], pair[...], 1, 0)
    total = total + got[...].astype(F32)
    keep[...] = total[:slab]
    for k, out in enumerate((s1, s2, s3)):
        out[...] = total[(k + 1) * slab : (k + 2) * slab].astype(BF16)


def last_kernel(keep_a, got_a, keep_b, g1, g2, g3, out):
    middle = keep_a.shape[1]
    out[:, :middle] = (keep_a[...] + got_a[...].astype(F32)).astype(BF16)
    total = keep_b[...]
    for got in (g1, g2, g3):
        total = total + got[...].astype(F32)
    out[:, middle:] = total.astype(BF16)


def line_kernel(blocks, out):
    total = blocks[0].astype(F32)
    for k in range(1, blocks.shape[0]):
        total = total + blocks[k].astype(F32)
    out[...] = total


def there_kernel(half, unit, head, later, out):
    out[...] = dot(unit[...], head[...], 1, 1).astype(BF16)


def here_kernel(half, unit, head, there, out):
    out[...] = (dot(unit[...], head[...], 1, 1) + there[...].astype(F32)).astype(BF16)


def gather_kernel(
    own_back, near_back, cross_back, far_back, own, near, cross, first, second, high, low
):
    far_turned = far_back[...].astype(F32).T.astype(BF16)
    total = (
        dot(own_back[...], own[...], 1, 0)
        + dot(near_back[...], near[...], 1, 0)
        + dot(cross_back[...], cross[...], 1, 0)
        + dot(far_turned, first[...], 1, 0)
        + dot(far_turned, second[...], 1, 0)
    )
    rounded = total.astype(BF16)
    high[...] = rounded
    low[...] = (total - rounded.astype(F32)).astype(BF16)


def pull_kernel(high, low, head, texts, inverses, pull, inner, column):
    step = pl.program_id(0)
    total = dot(high[...], head[...], 1, 0) + dot(low[...], head[...], 1, 0)
    pull[...] = total
    unit = texts[...].astype(F32) * inverses[:, 1:2]
    dots = jnp.sum(unit * total, axis=1, keepdims=True)

    @pl.when(step == 0)
    def _():
        column[...] = dots

    @pl.when(step > 0)
    def _():
        column[...] += dots

    @pl.when(step == pl.num_programs(0) - 1)
    def _():
        inner[...] = to_row(column[...])


def text_kernel(pull, texts, inverses, inner, there, out):
    inverse = inverses[:, 1:2]
    unit = texts[...].astype(F32) * inverse
    out[...] = ((pull[...] - unit * to_column(inner[...] + there[...])) * inverse).astype(BF16)


def per_device(images, texts, head, pair_mask, labels, logit_scale, logit_bias):
    rows, depth = images.shape
    width = texts.shape[1]
    steps = 4
    piece = width // steps
    me = lax.axis_index("dp")
    core = (me & 1)[None]
    where = jnp.stack([me & 1, (me >> 4) & (XS - 1), me >> 6])
    half = lax.axis_index("tensor")[None]
    labels = labels.reshape(1, rows)
    tile, square = (rows + EXTRA, rows), (rows, rows)

    near_text = send(texts, lambda i: i + 2)
    near_image = send(images, lambda i: i - 2)
    count = YS * XS * ZS * CORES
    odd_up = [(i, (i + 1) % count) for i in range(1, count, 2)]
    even_up = [(i, i + 1) for i in range(0, count, 2)]
    odd_down = [(i, i - 1) for i in range(1, count, 2)]
    even_down = [(i, (i - 1) % count) for i in range(0, count, 2)]

    mine, theirs = call(
        turned_kernel,
        [((depth // CORES, rows), BF16, whole((depth // CORES, rows)))] * 2,
        [SCALAR, whole((rows, depth))],
        (where, images),
        scratch=[pltpu.VMEM((depth, rows), BF16)],
    )
    theirs = send(theirs, other_core)

    projected, projected_b, own_part, own_sent, own_squares = call(
        project_kernel,
        [
            ((rows, width), F32, strip(rows, piece)),
            ((rows, width), BF16, strip(rows, piece)),
            (square, F32, whole(square)),
            (tile, BF16, whole(tile)),
            ((8, rows), F32, whole((8, rows))),
        ],
        [whole((rows, depth)), strip(depth, piece), strip(rows, piece)],
        (images, head, texts),
        grid=(steps,),
        scratch=[pltpu.VMEM((rows, 128), F32)],
    )
    far_second = lax.ppermute(texts, "dp", even_up)
    far_image_second = lax.ppermute(images, "dp", odd_down)
    near_text = gate(near_text, own_sent, theirs, mine)
    near_image = gate(near_image, far_second, far_image_second)
    far_first = lax.ppermute(near_text, "dp", odd_up)
    cross_text = send(near_text, other_core)
    far_image_first = lax.ppermute(near_image, "dp", even_down)
    cross_image = send(near_image, other_core)

    full = whole((rows, width))
    tile_outs = [
        (square, F32, whole(square)),
        (tile, BF16, whole(tile)),
        ((8, rows), F32, whole((8, rows))),
    ]
    pair_out = ((2, *tile), BF16, whole((2, *tile)))
    near_part, near_sent, near_squares = call(
        near_kernel,
        [tile_outs[0], pair_out, tile_outs[2]],
        [full, full, whole(tile)],
        (projected_b, near_text, own_sent),
    )
    near_there = swap_tensor(near_sent)
    cross_part, cross_sent, cross_squares = call(
        tile_kernel, tile_outs, [full, full], (projected_b, cross_text)
    )
    cross_there = swap_tensor(cross_sent)
    far_text, far_part, far_sent, far_squares = call(
        far_kernel,
        [((rows, width), BF16, full)] + tile_outs,
        [SCALAR, full, full, full],
        (core, projected_b, far_first, far_second),
    )
    far_there = swap_tensor(far_sent)

    scalars = [SCALAR] * 4
    known = (core, logit_scale, logit_bias, pair_mask, labels)
    halves = 2
    wide = width // halves
    some_pull, own_back, near_back, cross_back, inner, inverses = call(
        some_kernel,
        [
            ((rows, width), F32, strip(rows, wide)),
            (square, BF16, whole(square)),
            (square, BF16, whole(square)),
            (square, BF16, whole(square)),
            ((rows, 1), F32, whole((rows, 1))),
            ((rows, 2), F32, whole((rows, 2))),
        ],
        scalars
        + [whole((1, rows))]
        + [whole(square), whole((8, rows))]
        + [whole(square), whole((2, *tile)), whole((8, rows))]
        + [whole(square), whole(tile), whole((8, rows))]
        + [strip(rows, wide)] * 3
        + [LATER],
        known
        + (own_part, own_squares, near_part, near_there, near_squares)
        + (cross_part, cross_there, cross_squares)
        + (texts, near_text, cross_text, far_sent),
        grid=(halves,),
        scratch=[pltpu.VMEM((3, *square), BF16)],
    )
    grad_unit, far_back = call(
        unit_kernel,
        [((rows, width), BF16, strip(rows, wide)), (square, BF16, whole(square))],
        scalars
        + [whole((1, rows)), whole(square), whole(tile), whole((8, rows))]
        + [strip(rows, wide), strip(rows, wide), whole((rows, 1)), whole((rows, 2))]
        + [strip(rows, wide), LATER, LATER],
        known
        + (far_part, far_there, far_squares, far_text, some_pull, inner, inverses, projected)
        + (far_image_first, cross_image),
        grid=(halves,),
        scratch=[pltpu.VMEM(square, BF16), pltpu.VMEM((rows, 1), F32)],
    )

    grad_pair = send(grad_unit, other_core)
    lines = depth // CORES
    parts_of = 2 * halves
    slab = width // parts_of
    first_half = lambda j: (0, jnp.minimum(j, halves - 1))
    second_half = lambda j: (0, jnp.maximum(j - halves, 0))
    a_spec = pl.BlockSpec((lines // XS, slab), first_half)
    b_spec = pl.BlockSpec((lines // YS, slab), second_half)
    a_shape, b_shape = (lines // XS, width // 2), (lines // YS, width // 2)
    sides = (mine, theirs, grad_unit, grad_pair)
    side_specs = [whole((lines, rows))] * 2
    send_1, send_2, send_3, send_b = call(
        send_kernel,
        [(a_shape, BF16, a_spec)] * 3 + [(b_shape, BF16, b_spec)],
        side_specs + [strip(rows, slab)] * 2,
        sides,
        grid=(parts_of,),
        scratch=[pltpu.VMEM((lines // XS * (XS - 1), rows), BF16)] * 2,
    )
    got_b = send(send_b, over_y)
    gots_a = [send(block, over_x(d)) for d, block in ((2, send_2), (1, send_1), (3, send_3))]

    span = depth // 2
    chunk = span // steps

    def image_call(kernel, dtype, other, extra, operands):
        return pl.pallas_call(
            kernel,
            out_shape=jax.ShapeDtypeStruct((rows, span), dtype),
            grid_spec=pltpu.PrefetchScalarGridSpec(
                num_scalar_prefetch=1,
                grid=(steps,),
                in_specs=[
                    pl.BlockSpec((rows, width), lambda j, half: (0, 0)),
                    pl.BlockSpec((chunk, width), lambda j, half: ((half[0] ^ other) * steps + j, 0)),
                ]
                + extra,
                out_specs=pl.BlockSpec((rows, chunk), lambda j, half: (0, j)),
            ),
            compiler_params=pltpu.CompilerParams(vmem_limit_bytes=48 * 1024 * 1024),
        )(half, *operands)

    there = image_call(there_kernel, BF16, 1, [LATER], (grad_unit, head, send_b))

    near_back = send(gate(near_back, send_b), lambda i: i - 2)
    cross_back = send(gate(cross_back, send_b), lambda i: i - 3 if i % 2 else i - 1)
    far_back = send(gate(far_back, send_b), lambda i: i - 1 if i % 2 else i - 3)
    deep = depth // halves
    high, low = call(
        gather_kernel,
        [((rows, depth), BF16, strip(rows, deep))] * 2,
        [whole(square)] * 4 + [strip(rows, deep)] * 5,
        (own_back, near_back, cross_back, far_back)
        + (images, near_image, cross_image, far_image_first, far_image_second),
        grid=(halves,),
    )
    text_pull, dot_text = call(
        pull_kernel,
        [((rows, width), F32, strip(rows, piece)), ((1, rows), F32, whole((1, rows)))],
        [whole((rows, depth))] * 2
        + [strip(depth, piece), strip(rows, piece), whole((rows, 2))],
        (high, low, head, texts, inverses),
        grid=(steps,),
        scratch=[pltpu.VMEM((rows, 1), F32)],
    )
    gots_a[2] = gate(gots_a[2], high)
    short = lines // (YS * XS)
    keep_shape, keep_spec = (short, width // 2), strip(short, slab)
    keep_a, sent_a = call(
        sum_a_kernel,
        [(keep_shape, F32, keep_spec), (keep_shape, BF16, keep_spec)],
        side_specs + [strip(rows, slab)] * 2 + [strip(lines // XS, slab)] * 3,
        (*sides, *gots_a),
        grid=(halves,),
    )
    got_a = send(sent_a, over_y)
    second = pl.BlockSpec((rows, slab), lambda j: (0, j + halves))
    keep_b, *sends_b = call(
        sum_b_kernel,
        [(keep_shape, F32, keep_spec)] + [(keep_shape, BF16, keep_spec)] * 3,
        side_specs + [second] * 2 + [strip(lines // YS, slab), LATER],
        (*sides, got_b, sent_a),
        grid=(halves,),
    )
    gots_b = [send(sends_b[d - 1], over_x(d)) for d in (2, 1, 3)]
    there = swap_tensor(gate(there, keep_b))
    dot_there = swap_tensor(dot_text)
    gots_b[2] = gate(gots_b[2], text_pull)
    last = call(
        last_kernel,
        [((short, width), BF16, whole((short, width)))],
        [whole(keep_shape)] * 6,
        (keep_a, got_a, keep_b, *gots_b),
    )[0]
    last = gate(last, there, dot_there).reshape(ZS, short // ZS, width)
    line = [
        [index_of(y, x, z, c) for z in range(ZS)]
        for y in range(YS)
        for x in range(XS)
        for c in range(CORES)
    ]
    last = lax.all_to_all(last, "dp", 0, 0, axis_index_groups=line, tiled=True)
    grad_head = call(
        line_kernel,
        [((short // ZS, width), F32, whole((short // ZS, width)))],
        [whole(last.shape)],
        (last,),
    )[0]
    piece_spec = pl.BlockSpec((rows, chunk), lambda j, half: (0, j))
    grad_images = image_call(here_kernel, BF16, 0, [piece_spec], (grad_unit, head, there))

    grad_texts = call(
        text_kernel,
        [((rows, width), BF16, strip(rows, piece))],
        [strip(rows, piece)] * 2 + [whole((rows, 2)), whole((1, rows)), whole((1, rows))],
        (text_pull, texts, inverses, dot_text, dot_there),
        grid=(steps,),
    )[0]
    return (grad_images, grad_texts, grad_head)


def solution(mesh):
    return jax.shard_map(
        per_device,
        mesh=mesh,
        in_specs=(
            P("dp", None),
            P("dp", "tensor"),
            P(None, "tensor"),
            P("dp", None),
            P("dp"),
            P(),
            P(),
        ),
        out_specs=(P("dp", "tensor"), P("dp", "tensor"), P("dp", "tensor")),
        check_vma=False,
    )
```

profile of v0, /device:TPU:1, one launch (start us, length us, event | category | flops | bytes accessed | tf_op | source)
XLA Modules:
  0.0 164.0 jit_solution(9850504325905885263)
XLA Ops:
  0.6 2.5 %collective-permute-start = (bf16[256,2048]{1,0:T(8,128)(2,1)}, bf16[256,2048]{1,0:T(8,128)(2,1)S(1)}, u32[]{:S(2)}, u32[]{:S(2)}) collective-permute-start(bf16[256,2048]{1,0:T(8,128)(2,1)} %texts.7), channel_id=1, source_target_pairs={{0,4},{2,6},{4,8},{6,10},{8,12},{10,14},{12,16},{14,18},{16,20},{1... | collective-permute-start | bytes 3145736 | tf_op jit(solution)/shard_map/ppermute | solution.py:29
  4.5 3.2 %collective-permute-start.9 = (bf16[256,2048]{1,0:T(8,128)(2,1)}, bf16[256,2048]{1,0:T(8,128)(2,1)S(1)}, u32[]{:S(2)}, u32[]{:S(2)}) collective-permute-start(bf16[256,2048]{1,0:T(8,128)(2,1)} %own.1), channel_id=1, source_target_pairs={{2,0},{6,4},{10,8},{14,12},{18,16},{22,20},{26,24},{30,28},{34,32}... | collective-permute-start | bytes 3145736 | tf_op jit(solution)/shard_map/ppermute | solution.py:450
  7.6 7.2 %collective-permute-start.8 = (bf16[256,2048]{1,0:T(8,128)(2,1)}, bf16[256,2048]{1,0:T(8,128)(2,1)}, u32[]{:S(2)}, u32[]{:S(2)}) collective-permute-start(bf16[256,2048]{1,0:T(8,128)(2,1)} %own.1), channel_id=1, source_target_pairs={{0,252},{2,254},{4,0},{6,2},{8,4},{10,6},{12,8},{14,10},{16,12},{1... | collective-permute-start | bytes 3145736 | tf_op jit(solution)/shard_map/ppermute | solution.py:29
  18.6 6.5 %shard_map.94 = (f32[256,2048]{1,0:T(8,128)S(1)}, bf16[256,2048]{1,0:T(8,128)(2,1)S(1)}, f32[256,256]{1,0:T(8,128)S(1)}, bf16[272,256]{1,0:T(8,128)(2,1)S(1)}, f32[8,256]{1,0:T(8,128)S(1)}) custom-call(bf16[256,2048]{1,0:T(8,128)(2,1)S(1)} %copy-done.4, bf16[2048,2048]{1,0:T(8,128)(2,1)} %head.7, bf16[256,2048]{1,0:T(8,128)(2,1)S(1)} %copy-done), custom_call_target="tpu_custom_call" | custom-call | tf_op jit(solution)/shard_map/pallas_call | solution.py:86
  25.2 8.3 %collective-permute-done.refs_0_ = bf16[256,2048]{1,0:T(8,128)(2,1)S(1)} collective-permute-done((bf16[256,2048]{1,0:T(8,128)(2,1)}, bf16[256,2048]{1,0:T(8,128)(2,1)S(1)}, u32[]{:S(2)}, u32[]{:S(2)}) %collective-permute-start) | collective-permute-done | bytes 1048608 | tf_op jit(solution)/shard_map/ppermute | solution.py:29
  36.0 1.9 %collective-permute-done.8.refs_0_ = bf16[256,2048]{1,0:T(8,128)(2,1)} collective-permute-done((bf16[256,2048]{1,0:T(8,128)(2,1)}, bf16[256,2048]{1,0:T(8,128)(2,1)}, u32[]{:S(2)}, u32[]{:S(2)}) %collective-permute-start.8) | collective-permute-done | bytes 1048608 | tf_op jit(solution)/shard_map/ppermute | solution.py:29
  39.2 7.4 %collective-permute-start.11 = (bf16[256,2048]{1,0:T(8,128)(2,1)}, bf16[256,2048]{1,0:T(8,128)(2,1)S(1)}, u32[]{:S(2)}, u32[]{:S(2)}) collective-permute-start(bf16[256,2048]{1,0:T(8,128)(2,1)} %shard_map.101.near), channel_id=1, source_target_pairs={{0,2},{2,0},{4,6},{6,4},{8,10},{10,8},{12,14},{14,12},{16,18},{18,... | collective-permute-start | bytes 3145736 | tf_op jit(solution)/shard_map/ppermute | solution.py:29
  47.2 2.7 %collective-permute-start.5 = (bf16[2,272,256]{2,1,0:T(8,128)(2,1)S(1)}, bf16[2,272,256]{2,1,0:T(8,128)(2,1)S(1)}, u32[]{:S(2)}, u32[]{:S(2)}) collective-permute-start(bf16[2,272,256]{2,1,0:T(8,128)(2,1)S(1)} %get-tuple-element.53), channel_id=1, source_target_pairs={{0,1},{1,0},{2,3},{3,2},{4,5},{5,4},{6,7},{7,6},{8,9},{9,8},{10,11... | collective-permute-start | bytes 835592 | tf_op jit(solution)/shard_map/ppermute | solution.py:33
  51.6 2.7 %collective-permute-start.4 = (bf16[272,256]{1,0:T(8,128)(2,1)S(1)}, bf16[272,256]{1,0:T(8,128)(2,1)S(1)}, u32[]{:S(2)}, u32[]{:S(2)}) collective-permute-start(bf16[272,256]{1,0:T(8,128)(2,1)S(1)} %get-tuple-element.47.later), channel_id=1, source_target_pairs={{0,1},{1,0},{2,3},{3,2},{4,5},{5,4},{6,7},{7,6},{8,9},{9,8},{10,11... | collective-permute-start | bytes 417800 | tf_op jit(solution)/shard_map/ppermute | solution.py:33
  55.6 6.5 %collective-permute-done.5.near_there = bf16[2,272,256]{2,1,0:T(8,128)(2,1)S(1)} collective-permute-done((bf16[2,272,256]{2,1,0:T(8,128)(2,1)S(1)}, bf16[2,272,256]{2,1,0:T(8,128)(2,1)S(1)}, u32[]{:S(2)}, u32[]{:S(2)}) %collective-permute-start.5) | collective-permute-done | bytes 278560 | tf_op jit(solution)/shard_map/ppermute | solution.py:33
  62.1 3.0 %collective-permute-done.7.cross_there = bf16[272,256]{1,0:T(8,128)(2,1)S(1)} collective-permute-done((bf16[272,256]{1,0:T(8,128)(2,1)S(1)}, bf16[272,256]{1,0:T(8,128)(2,1)S(1)}, u32[]{:S(2)}, u32[]{:S(2)}) %collective-permute-start.7) | collective-permute-done | bytes 139296 | tf_op jit(solution)/shard_map/ppermute | solution.py:33
  65.1 3.6 %shard_map.100 = (f32[256,2048]{1,0:T(8,128)}, bf16[256,256]{1,0:T(8,128)(2,1)S(1)}, bf16[256,256]{1,0:T(8,128)(2,1)S(1)}, bf16[256,256]{1,0:T(8,128)(2,1)S(1)},...) custom-call(s32[1]{0:T(128)} %bitcast.1.core, f32[1]{0:T(128)S(6)} %copy.28.scale, f32[1]{0:T(128)S(6)} %copy.29.bias, ...), custom_call_target="tpu_custom_call" | custom-call | tf_op jit(solution)/shard_map/pallas_call | solution.py:86
  68.8 3.4 %shard_map.102 = (bf16[256,2048]{1,0:T(8,128)(2,1)S(1)}, bf16[256,256]{1,0:T(8,128)(2,1)S(1)}) custom-call(s32[1]{0:T(128)} %bitcast.1.core, f32[1]{0:T(128)S(6)} %copy.28.scale, f32[1]{0:T(128)S(6)} %copy.29.bias, s32[1,4]{1,0:T(1,128)S(1)} %copy-done.22, s32[1,256]{1,0:T(1,128)S(1)} %bitcast.7, f32[256,256]{1,0:T(8,128)S(1)} %get-tuple-element.46.part, ...), custom_call_target="tpu_custom_call" | custom-call | tf_op jit(solution)/shard_map/pallas_call | solution.py:86
  72.8 2.3 %collective-permute-done.12.pair = bf16[256,2048]{1,0:T(8,128)(2,1)S(1)} collective-permute-done((bf16[256,2048]{1,0:T(8,128)(2,1)S(1)}, bf16[256,2048]{1,0:T(8,128)(2,1)S(1)}, u32[]{:S(2)}, u32[]{:S(2)}) %collective-permute-start.12) | collective-permute-done | bytes 1048608 | tf_op jit(solution)/shard_map/ppermute | solution.py:29
  75.1 3.7 %shard_map.103 = (bf16[256,1024]{1,0:T(8,128)(2,1)}, bf16[256,1024]{1,0:T(8,128)(2,1)}, bf16[256,1024]{1,0:T(8,128)(2,1)}, bf16[512,1024]{1,0:T(8,128)(2,1)S(1)}) custom-call(bf16[1024,256]{1,0:T(8,128)(2,1)S(1)} %get-tuple-element.45.refs_3_.mine, bf16[1024,256]{1,0:T(8,128)(2,1)S(1)} %collective-permute-done.1.refs_2_.theirs, ...), custom_call_target="tpu_custom_call" | custom-call | tf_op jit(solution)/shard_map/pallas_call | solution.py:86
  79.2 1.5 collective-permute-start.15
  81.8 4.5 %collective-permute-done.19.far_back = bf16[256,256]{1,0:T(8,128)(2,1)S(1)} collective-permute-done((bf16[256,256]{1,0:T(8,128)(2,1)S(1)}, bf16[256,256]{1,0:T(8,128)(2,1)S(1)}, u32[]{:S(2)}, u32[]{:S(2)}) %collective-permute-start.19) | collective-permute-done | bytes 131104 | tf_op jit(solution)/shard_map/ppermute | solution.py:29
  86.3 5.2 %collective-permute-start.18 = (bf16[256,256]{1,0:T(8,128)(2,1)S(1)}, bf16[256,256]{1,0:T(8,128)(2,1)S(1)}, u32[]{:S(2)}, u32[]{:S(2)}) collective-permute-start(bf16[256,256]{1,0:T(8,128)(2,1)S(1)} %shard_map.106), channel_id=1, source_target_pairs={{0,254},{2,252},{4,2},{6,0},{8,6},{10,4},{12,10},{14,8},{16,14},{1... | collective-permute-start | bytes 393224 | tf_op jit(solution)/shard_map/ppermute | solution.py:29
  91.5 3.4 %collective-permute-done.18.cross_back = bf16[256,256]{1,0:T(8,128)(2,1)S(1)} collective-permute-done((bf16[256,256]{1,0:T(8,128)(2,1)S(1)}, bf16[256,256]{1,0:T(8,128)(2,1)S(1)}, u32[]{:S(2)}, u32[]{:S(2)}) %collective-permute-start.18) | collective-permute-done | bytes 131104 | tf_op jit(solution)/shard_map/ppermute | solution.py:29
  95.6 12.0 %collective-permute-start.17 = (bf16[256,256]{1,0:T(8,128)(2,1)S(1)}, bf16[256,256]{1,0:T(8,128)(2,1)}, u32[]{:S(2)}, u32[]{:S(2)}) collective-permute-start(bf16[256,256]{1,0:T(8,128)(2,1)S(1)} %shard_map.105), channel_id=1, source_target_pairs={{0,252},{2,254},{4,0},{6,2},{8,4},{10,6},{12,8},{14,10},{16,12},{1... | collective-permute-start | bytes 393224 | tf_op jit(solution)/shard_map/ppermute | solution.py:29
  107.6 4.2 %shard_map.104.refs_0_ = bf16[256,1024]{1,0:T(8,128)(2,1)S(1)} custom-call(s32[1]{0:T(128)} %bitcast.half, bf16[256,2048]{1,0:T(8,128)(2,1)S(1)} %get-tuple-element.62.own.unit, bf16[2048,2048]{1,0:T(8,128)(2,1)} %head.7, bf16[512,1024]{1,0:T(8,128)(2,1)S(1)} %get-tuple-element.63.later.refs_1_), custom_call_target="tpu_custom_call" | custom-call | tf_op jit(solution)/shard_map/pallas_call | solution.py:552
  111.8 3.3 %shard_map.108 = (bf16[256,2048]{1,0:T(8,128)(2,1)S(1)}, bf16[256,2048]{1,0:T(8,128)(2,1)S(1)}) custom-call(bf16[256,256]{1,0:T(8,128)(2,1)S(1)} %get-tuple-element.67.own_back, bf16[256,256]{1,0:T(8,128)(2,1)} %collective-permute-done.17.near_back, bf16[256,256]{1,0:T(8,128)(2,1)S(1)} %copy-done.20, bf16[256,256]{1,0:T(8,128)(2,1)S(1)} %copy-done.18, ...), custom_call_target="tpu_custom_call" | custom-call | tf_op jit(solution)/shard_map/pallas_call | solution.py:86
  116.7 1.9 %shard_map.110 = (f32[128,1024]{1,0:T(8,128)S(1)}, bf16[128,1024]{1,0:T(8,128)(2,1)S(1)}) custom-call(bf16[1024,256]{1,0:T(8,128)(2,1)S(1)} %copy-done.7, bf16[1024,256]{1,0:T(8,128)(2,1)S(1)} %copy-done.9, bf16[256,2048]{1,0:T(8,128)(2,1)S(1)} %get-tuple-element.62.own.unit, bf16[256,2048]{1,0:T(8,128)(2,1)S(1)} %copy-done.3, ...), custom_call_target="tpu_custom_call" | custom-call | tf_op jit(solution)/shard_map/pallas_call | solution.py:86
  118.6 2.1 %shard_map.111 = (f32[128,1024]{1,0:T(8,128)S(1)}, bf16[128,1024]{1,0:T(8,128)(2,1)S(1)}, bf16[128,1024]{1,0:T(8,128)(2,1)S(1)}, bf16[128,1024]{1,0:T(8,128)(2,1)S(1)}) custom-call(bf16[1024,256]{1,0:T(8,128)(2,1)S(1)} %copy-done.7, bf16[1024,256]{1,0:T(8,128)(2,1)S(1)} %copy-done.9, bf16[256,2048]{1,0:T(8,128)(2,1)S(1)} %get-tuple-element.62.own.unit, ...), custom_call_target="tpu_custom_call" | custom-call | tf_op jit(solution)/shard_map/pallas_call | solution.py:86
  120.7 3.4 %collective-permute-start.20 = (bf16[256,1024]{1,0:T(8,128)(2,1)S(1)}, bf16[256,1024]{1,0:T(8,128)(2,1)S(1)}, u32[]{:S(2)}, u32[]{:S(2)}) collective-permute-start(bf16[256,1024]{1,0:T(8,128)(2,1)S(1)} %shard_map.112), channel_id=1, source_target_pairs={{0,1},{1,0},{2,3},{3,2},{4,5},{5,4},{6,7},{7,6},{8,9},{9,8},{10,11... | collective-permute-start | bytes 1572872 | tf_op jit(solution)/shard_map/ppermute | solution.py:33
  126.5 7.5 %shard_map.114 = (f32[256,2048]{1,0:T(8,128)S(1)}, f32[1,256]{1,0:T(1,128)S(1)}) custom-call(bf16[256,2048]{1,0:T(8,128)(2,1)S(1)} %get-tuple-element.71.refs_1_.high, bf16[256,2048]{1,0:T(8,128)(2,1)S(1)} %get-tuple-element.74.low, bf16[2048,2048]{1,0:T(8,128)(2,1)} %head.7, bf16[256,2048]{1,0:T(8,128)(2,1)S(1)} %copy-done.1, ...), custom_call_target="tpu_custom_call" | custom-call | tf_op jit(solution)/shard_map/pallas_call | solution.py:86
  135.4 2.1 %collective-permute-done.22.got_a = bf16[128,1024]{1,0:T(8,128)(2,1)S(1)} collective-permute-done((bf16[128,1024]{1,0:T(8,128)(2,1)S(1)}, bf16[128,1024]{1,0:T(8,128)(2,1)S(1)}, u32[]{:S(2)}, u32[]{:S(2)}) %collective-permute-start.22) | collective-permute-done | bytes 262176 | tf_op jit(solution)/shard_map/ppermute | solution.py:29
  138.4 6.9 %all-to-all-start = ((bf16[8,16,2048]{2,1,0:T(8,128)(2,1)}), bf16[8,16,2048]{2,1,0:T(8,128)(2,1)S(1)}, u32[]{:S(2)}, u32[]{:S(2)}) async-start(bf16[8,16,2048]{2,1,0:T(8,128)(2,1)} %bitcast.5), calls=%async_computation | async-start | bytes 1048576 | tf_op jit(solution)/shard_map/all_to_all | solution.py:627
  145.4 1.6 copy-done.11
  146.9 2.2 %shard_map.115 = bf16[256,2048]{1,0:T(8,128)(2,1)} custom-call(f32[256,2048]{1,0:T(8,128)S(1)} %copy-done.11, bf16[256,2048]{1,0:T(8,128)(2,1)S(1)} %copy-done.1, f32[256,2]{1,0:T(8,128)S(1)} %get-tuple-element.60.inverses, f32[1,256]{1,0:T(1,128)S(1)} %get-tuple-element.76.inner, f32[1,256]{1,0:T(1,128)S(1)} %collective-permute-done.21.there.refs_2_), custom_call_target="tpu_custom_call" | custom-call | tf_op jit(solution)/shard_map/pallas_call | solution.py:86
  149.1 4.8 %shard_map.113 = bf16[256,1024]{1,0:T(8,128)(2,1)} custom-call(s32[1]{0:T(128)} %bitcast.half, bf16[256,2048]{1,0:T(8,128)(2,1)S(1)} %get-tuple-element.62.own.unit, bf16[2048,2048]{1,0:T(8,128)(2,1)} %head.7, bf16[256,1024]{1,0:T(8,128)(2,1)S(1)} %collective-permute-done.20.there.refs_1_), custom_call_target="tpu_custom_call" | custom-call | tf_op jit(solution)/shard_map/pallas_call | solution.py:552
  153.9 9.4 %all-to-all-done.blocks = bf16[8,16,2048]{2,1,0:T(8,128)(2,1)S(1)} async-done(((bf16[8,16,2048]{2,1,0:T(8,128)(2,1)}), bf16[8,16,2048]{2,1,0:T(8,128)(2,1)S(1)}, u32[]{:S(2)}, u32[]{:S(2)}) %all-to-all-start) | async-done | bytes 524320 | tf_op jit(solution)/shard_map/all_to_all | solution.py:627
  (95 shorter events, 20.8 us)
Async XLA Ops:
  0.6 32.8 %collective-permute-start = (bf16[256,2048]{1,0:T(8,128)(2,1)}, bf16[256,2048]{1,0:T(8,128)(2,1)S(1)}, u32[]{:S(2)}, u32[]{:S(2)}) collective-permute-start(bf16[256,2048]{1,0:T(8,128)(2,1)} %texts.7), channel_id=1, source_target_pairs={{0,4},{2,6},{4,8},{6,10},{8,12},{10,14},{12,16},{14,18},{16,20},{1... | collective-permute-start | bytes 3145736 | tf_op jit(solution)/shard_map/ppermute | solution.py:29
  3.2 32.8 %collective-permute-start.3 = (bf16[256,2048]{1,0:T(8,128)(2,1)}, bf16[256,2048]{1,0:T(8,128)(2,1)S(1)}, u32[]{:S(2)}, u32[]{:S(2)}) collective-permute-start(bf16[256,2048]{1,0:T(8,128)(2,1)} %texts.7), channel_id=1, source_target_pairs={{0,2},{4,6},{8,10},{12,14},{16,18},{20,22},{24,26},{28,30},{32,34}... | collective-permute-start | bytes 3145736 | tf_op jit(solution)/shard_map/ppermute | solution.py:449
  4.5 31.6 %collective-permute-start.9 = (bf16[256,2048]{1,0:T(8,128)(2,1)}, bf16[256,2048]{1,0:T(8,128)(2,1)S(1)}, u32[]{:S(2)}, u32[]{:S(2)}) collective-permute-start(bf16[256,2048]{1,0:T(8,128)(2,1)} %own.1), channel_id=1, source_target_pairs={{2,0},{6,4},{10,8},{14,12},{18,16},{22,20},{26,24},{30,28},{34,32}... | collective-permute-start | bytes 3145736 | tf_op jit(solution)/shard_map/ppermute | solution.py:450
  7.6 30.3 %collective-permute-start.8 = (bf16[256,2048]{1,0:T(8,128)(2,1)}, bf16[256,2048]{1,0:T(8,128)(2,1)}, u32[]{:S(2)}, u32[]{:S(2)}) collective-permute-start(bf16[256,2048]{1,0:T(8,128)(2,1)} %own.1), channel_id=1, source_target_pairs={{0,252},{2,254},{4,0},{6,2},{8,4},{10,6},{12,8},{14,10},{16,12},{1... | collective-permute-start | bytes 3145736 | tf_op jit(solution)/shard_map/ppermute | solution.py:29
  17.2 57.9 %copy-start.6 = (bf16[1024,256]{1,0:T(8,128)(2,1)}, bf16[1024,256]{1,0:T(8,128)(2,1)S(1)}, u32[]{:S(2)}) copy-start(bf16[1024,256]{1,0:T(8,128)(2,1)S(1)} %get-tuple-element.45.refs_3_.mine) | copy-start | bytes 1572868
  17.2 8.0 %collective-permute-start.1 = (bf16[1024,256]{1,0:T(8,128)(2,1)S(1)}, bf16[1024,256]{1,0:T(8,128)(2,1)S(1)}, u32[]{:S(2)}, u32[]{:S(2)}) collective-permute-start(bf16[1024,256]{1,0:T(8,128)(2,1)S(1)} %get-tuple-element.44), channel_id=1, source_target_pairs={{0,2},{2,0},{4,6},{6,4},{8,10},{10,8},{12,14},{14,12},{16,18},{18,... | collective-permute-start | bytes 1572872 | tf_op jit(solution)/shard_map/ppermute | solution.py:29
  25.2 49.9 %copy-start.8 = (bf16[1024,256]{1,0:T(8,128)(2,1)}, bf16[1024,256]{1,0:T(8,128)(2,1)S(1)}, u32[]{:S(2)}) copy-start(bf16[1024,256]{1,0:T(8,128)(2,1)S(1)} %collective-permute-done.1.refs_2_.theirs) | copy-start | bytes 1572868
  33.4 16.5 %collective-permute-start.6 = (bf16[256,2048]{1,0:T(8,128)(2,1)S(1)}, bf16[256,2048]{1,0:T(8,128)(2,1)S(1)}, u32[]{:S(2)}, u32[]{:S(2)}) collective-permute-start(bf16[256,2048]{1,0:T(8,128)(2,1)S(1)} %shard_map.96.text.near), channel_id=1, source_target_pairs={{0,2},{2,0},{4,6},{6,4},{8,10},{10,8},{12,14},{14,12},{16,18},{18,... | collective-permute-start | bytes 3145736 | tf_op jit(solution)/shard_map/ppermute | solution.py:29
  34.6 16.3 %collective-permute-start.2 = (bf16[256,2048]{1,0:T(8,128)(2,1)S(1)}, bf16[256,2048]{1,0:T(8,128)(2,1)S(1)}, u32[]{:S(2)}, u32[]{:S(2)}) collective-permute-start(bf16[256,2048]{1,0:T(8,128)(2,1)S(1)} %shard_map.96.text.near), channel_id=1, source_target_pairs={{2,4},{6,8},{10,12},{14,16},{18,20},{22,24},{26,28},{30,32},{34,36... | collective-permute-start | bytes 3145736 | tf_op jit(solution)/shard_map/ppermute | solution.py:453
  38.0 30.8 %collective-permute-start.10 = (bf16[256,2048]{1,0:T(8,128)(2,1)}, bf16[256,2048]{1,0:T(8,128)(2,1)S(1)}, u32[]{:S(2)}, u32[]{:S(2)}) collective-permute-start(bf16[256,2048]{1,0:T(8,128)(2,1)} %shard_map.101.near), channel_id=1, source_target_pairs={{0,254},{4,2},{8,6},{12,10},{16,14},{20,18},{24,22},{28,26},{32,30... | collective-permute-start | bytes 3145736 | tf_op jit(solution)/shard_map/ppermute | solution.py:455
  39.2 29.5 %collective-permute-start.11 = (bf16[256,2048]{1,0:T(8,128)(2,1)}, bf16[256,2048]{1,0:T(8,128)(2,1)S(1)}, u32[]{:S(2)}, u32[]{:S(2)}) collective-permute-start(bf16[256,2048]{1,0:T(8,128)(2,1)} %shard_map.101.near), channel_id=1, source_target_pairs={{0,2},{2,0},{4,6},{6,4},{8,10},{10,8},{12,14},{14,12},{16,18},{18,... | collective-permute-start | bytes 3145736 | tf_op jit(solution)/shard_map/ppermute | solution.py:29
  47.2 15.0 %collective-permute-start.5 = (bf16[2,272,256]{2,1,0:T(8,128)(2,1)S(1)}, bf16[2,272,256]{2,1,0:T(8,128)(2,1)S(1)}, u32[]{:S(2)}, u32[]{:S(2)}) collective-permute-start(bf16[2,272,256]{2,1,0:T(8,128)(2,1)S(1)} %get-tuple-element.53), channel_id=1, source_target_pairs={{0,1},{1,0},{2,3},{3,2},{4,5},{5,4},{6,7},{7,6},{8,9},{9,8},{10,11... | collective-permute-start | bytes 835592 | tf_op jit(solution)/shard_map/ppermute | solution.py:33
  50.4 14.7 %copy-start.1 = (bf16[256,2048]{1,0:T(8,128)(2,1)S(1)}, bf16[256,2048]{1,0:T(8,128)(2,1)}, u32[]{:S(2)}) copy-start(bf16[256,2048]{1,0:T(8,128)(2,1)} %texts.7) | copy-start | bytes 3145732
  50.5 14.7 %copy-start.21 = (s32[256]{0:T(256)S(1)}, s32[256]{0:T(256)}, u32[]{:S(2)}) copy-start(s32[256]{0:T(256)} %param.11) | copy-start | bytes 3076
  50.5 14.7 %copy-start.22 = (s32[1,4]{1,0:T(1,128)S(1)}, s32[1,4]{1,0:T(1,128)}, u32[]{:S(2)}) copy-start(s32[1,4]{1,0:T(1,128)} %mask.3) | copy-start | bytes 52
  50.5 14.6 %collective-permute-start.7 = (bf16[272,256]{1,0:T(8,128)(2,1)S(1)}, bf16[272,256]{1,0:T(8,128)(2,1)S(1)}, u32[]{:S(2)}, u32[]{:S(2)}) collective-permute-start(bf16[272,256]{1,0:T(8,128)(2,1)S(1)} %get-tuple-element.56), channel_id=1, source_target_pairs={{0,1},{1,0},{2,3},{3,2},{4,5},{5,4},{6,7},{7,6},{8,9},{9,8},{10,11... | collective-permute-start | bytes 417800 | tf_op jit(solution)/shard_map/ppermute | solution.py:33
  51.6 17.2 %collective-permute-start.4 = (bf16[272,256]{1,0:T(8,128)(2,1)S(1)}, bf16[272,256]{1,0:T(8,128)(2,1)S(1)}, u32[]{:S(2)}, u32[]{:S(2)}) collective-permute-start(bf16[272,256]{1,0:T(8,128)(2,1)S(1)} %get-tuple-element.47.later), channel_id=1, source_target_pairs={{0,1},{1,0},{2,3},{3,2},{4,5},{5,4},{6,7},{7,6},{8,9},{9,8},{10,11... | collective-permute-start | bytes 417800 | tf_op jit(solution)/shard_map/ppermute | solution.py:33
  72.2 2.9 %collective-permute-start.12 = (bf16[256,2048]{1,0:T(8,128)(2,1)S(1)}, bf16[256,2048]{1,0:T(8,128)(2,1)S(1)}, u32[]{:S(2)}, u32[]{:S(2)}) collective-permute-start(bf16[256,2048]{1,0:T(8,128)(2,1)S(1)} %get-tuple-element.62.own.unit), channel_id=1, source_target_pairs={{0,2},{2,0},{4,6},{6,4},{8,10},{10,8},{12,14},{14,12},{16,18},{18,... | collective-permute-start | bytes 3145736 | tf_op jit(solution)/shard_map/ppermute | solution.py:29
  78.8 39.8 %collective-permute-start.13 = (bf16[512,1024]{1,0:T(8,128)(2,1)S(1)}, bf16[512,1024]{1,0:T(8,128)(2,1)}, u32[]{:S(2)}, u32[]{:S(2)}) collective-permute-start(bf16[512,1024]{1,0:T(8,128)(2,1)S(1)} %get-tuple-element.63.later.refs_1_), channel_id=1, source_target_pairs={{0,128},{2,130},{4,132},{6,134},{8,136},{10,138},{12,140},{14,142}... | collective-permute-start | bytes 3145736 | tf_op jit(solution)/shard_map/ppermute | solution.py:29
  79.2 36.0 %collective-permute-start.16 = (bf16[256,1024]{1,0:T(8,128)(2,1)}, bf16[256,1024]{1,0:T(8,128)(2,1)}, u32[]{:S(2)}, u32[]{:S(2)}) collective-permute-start(bf16[256,1024]{1,0:T(8,128)(2,1)} %get-tuple-element.66), channel_id=1, source_target_pairs={{0,96},{2,98},{4,100},{6,102},{8,104},{10,106},{12,108},{14,110},{... | collective-permute-start | bytes 1572872 | tf_op jit(solution)/shard_map/ppermute | solution.py:29
  79.2 36.0 %collective-permute-start.14 = (bf16[256,1024]{1,0:T(8,128)(2,1)}, bf16[256,1024]{1,0:T(8,128)(2,1)}, u32[]{:S(2)}, u32[]{:S(2)}) collective-permute-start(bf16[256,1024]{1,0:T(8,128)(2,1)} %get-tuple-element.64), channel_id=1, source_target_pairs={{0,64},{2,66},{4,68},{6,70},{8,72},{10,74},{12,76},{14,78},{16,80}... | collective-permute-start | bytes 1572872 | tf_op jit(solution)/shard_map/ppermute | solution.py:29
  79.2 36.0 %collective-permute-start.15 = (bf16[256,1024]{1,0:T(8,128)(2,1)}, bf16[256,1024]{1,0:T(8,128)(2,1)}, u32[]{:S(2)}, u32[]{:S(2)}) collective-permute-start(bf16[256,1024]{1,0:T(8,128)(2,1)} %get-tuple-element.65), channel_id=1, source_target_pairs={{0,32},{2,34},{4,36},{6,38},{8,40},{10,42},{12,44},{14,46},{16,48}... | collective-permute-start | bytes 1572872 | tf_op jit(solution)/shard_map/ppermute | solution.py:29
  80.6 5.7 %collective-permute-start.19 = (bf16[256,256]{1,0:T(8,128)(2,1)S(1)}, bf16[256,256]{1,0:T(8,128)(2,1)S(1)}, u32[]{:S(2)}, u32[]{:S(2)}) collective-permute-start(bf16[256,256]{1,0:T(8,128)(2,1)S(1)} %shard_map.107), channel_id=1, source_target_pairs={{0,250},{2,0},{4,254},{6,4},{8,2},{10,8},{12,6},{14,12},{16,10},{1... | collective-permute-start | bytes 393224 | tf_op jit(solution)/shard_map/ppermute | solution.py:29
  86.3 8.6 %collective-permute-start.18 = (bf16[256,256]{1,0:T(8,128)(2,1)S(1)}, bf16[256,256]{1,0:T(8,128)(2,1)S(1)}, u32[]{:S(2)}, u32[]{:S(2)}) collective-permute-start(bf16[256,256]{1,0:T(8,128)(2,1)S(1)} %shard_map.106), channel_id=1, source_target_pairs={{0,254},{2,252},{4,2},{6,0},{8,6},{10,4},{12,10},{14,8},{16,14},{1... | collective-permute-start | bytes 393224 | tf_op jit(solution)/shard_map/ppermute | solution.py:29
  95.6 16.2 %collective-permute-start.17 = (bf16[256,256]{1,0:T(8,128)(2,1)S(1)}, bf16[256,256]{1,0:T(8,128)(2,1)}, u32[]{:S(2)}, u32[]{:S(2)}) collective-permute-start(bf16[256,256]{1,0:T(8,128)(2,1)S(1)} %shard_map.105), channel_id=1, source_target_pairs={{0,252},{2,254},{4,0},{6,2},{8,4},{10,6},{12,8},{14,10},{16,12},{1... | collective-permute-start | bytes 393224 | tf_op jit(solution)/shard_map/ppermute | solution.py:29
  120.7 17.7 %collective-permute-start.20 = (bf16[256,1024]{1,0:T(8,128)(2,1)S(1)}, bf16[256,1024]{1,0:T(8,128)(2,1)S(1)}, u32[]{:S(2)}, u32[]{:S(2)}) collective-permute-start(bf16[256,1024]{1,0:T(8,128)(2,1)S(1)} %shard_map.112), channel_id=1, source_target_pairs={{0,1},{1,0},{2,3},{3,2},{4,5},{5,4},{6,7},{7,6},{8,9},{9,8},{10,11... | collective-permute-start | bytes 1572872 | tf_op jit(solution)/shard_map/ppermute | solution.py:33
  124.1 9.9 %collective-permute-start.25 = (bf16[128,1024]{1,0:T(8,128)(2,1)S(1)}, bf16[128,1024]{1,0:T(8,128)(2,1)S(1)}, u32[]{:S(2)}, u32[]{:S(2)}) collective-permute-start(bf16[128,1024]{1,0:T(8,128)(2,1)S(1)} %get-tuple-element.80), channel_id=1, source_target_pairs={{0,96},{2,98},{4,100},{6,102},{8,104},{10,106},{12,108},{14,110},{... | collective-permute-start | bytes 786440 | tf_op jit(solution)/shard_map/ppermute | solution.py:29
  124.1 13.3 %collective-permute-start.22 = (bf16[128,1024]{1,0:T(8,128)(2,1)S(1)}, bf16[128,1024]{1,0:T(8,128)(2,1)S(1)}, u32[]{:S(2)}, u32[]{:S(2)}) collective-permute-start(bf16[128,1024]{1,0:T(8,128)(2,1)S(1)} %get-tuple-element.72.later), channel_id=1, source_target_pairs={{0,128},{2,130},{4,132},{6,134},{8,136},{10,138},{12,140},{14,142}... | collective-permute-start | bytes 786440 | tf_op jit(solution)/shard_map/ppermute | solution.py:29
  125.0 12.4 %collective-permute-start.23 = (bf16[128,1024]{1,0:T(8,128)(2,1)S(1)}, bf16[128,1024]{1,0:T(8,128)(2,1)S(1)}, u32[]{:S(2)}, u32[]{:S(2)}) collective-permute-start(bf16[128,1024]{1,0:T(8,128)(2,1)S(1)} %get-tuple-element.78), channel_id=1, source_target_pairs={{0,64},{2,66},{4,68},{6,70},{8,72},{10,74},{12,76},{14,78},{16,80}... | collective-permute-start | bytes 786440 | tf_op jit(solution)/shard_map/ppermute | solution.py:29
  125.0 12.4 %collective-permute-start.24 = (bf16[128,1024]{1,0:T(8,128)(2,1)S(1)}, bf16[128,1024]{1,0:T(8,128)(2,1)S(1)}, u32[]{:S(2)}, u32[]{:S(2)}) collective-permute-start(bf16[128,1024]{1,0:T(8,128)(2,1)S(1)} %get-tuple-element.79), channel_id=1, source_target_pairs={{0,32},{2,34},{4,36},{6,38},{8,40},{10,42},{12,44},{14,46},{16,48}... | collective-permute-start | bytes 786440 | tf_op jit(solution)/shard_map/ppermute | solution.py:29
  134.0 4.4 %collective-permute-start.21 = (f32[1,256]{1,0:T(1,128)S(1)}, f32[1,256]{1,0:T(1,128)S(1)}, u32[]{:S(2)}, u32[]{:S(2)}) collective-permute-start(f32[1,256]{1,0:T(1,128)S(1)} %get-tuple-element.76.inner), channel_id=1, source_target_pairs={{0,1},{1,0},{2,3},{3,2},{4,5},{5,4},{6,7},{7,6},{8,9},{9,8},{10,11... | collective-permute-start | bytes 3080 | tf_op jit(solution)/shard_map/ppermute | solution.py:33
  138.4 24.9 %all-to-all-start = ((bf16[8,16,2048]{2,1,0:T(8,128)(2,1)}), bf16[8,16,2048]{2,1,0:T(8,128)(2,1)S(1)}, u32[]{:S(2)}, u32[]{:S(2)}) async-start(bf16[8,16,2048]{2,1,0:T(8,128)(2,1)} %bitcast.5), calls=%async_computation | async-start | bytes 1048576 | tf_op jit(solution)/shard_map/all_to_all | solution.py:627
  (18 other events, 74.7 us)
where the time goes:
time: 165 us; the launch traced here: 164 us
  starting transfers between devices  66.2 us (40%)
  Pallas kernels  47.6 us (29%)
  waiting for transfers between devices  41.4 us (25%)
  local copies, waits for them, and re-layouts  6.3 us (4%)
  between operations  2.35 us (1%)
    ppermute x17, starting transfers between devices, send(): return lax.ppermute(block, 'dp', route(target))  41.6 us
    pallas_call x15, Pallas kernels, call(): pl.pallas_call(kernel, out_shape=shapes, grid=grid or (1,), in_specs=ins,...  38.7 us
    ppermute x17, waiting for transfers between devices, send(): return lax.ppermute(block, 'dp', route(target))  22.5 us
    ppermute x5, starting transfers between devices, swap_tensor(): return lax.ppermute(block, 'tensor', [(0, 1), (1, 0)])  10.6 us
    ppermute x5, waiting for transfers between devices, swap_tensor(): return lax.ppermute(block, 'tensor', [(0, 1), (1, 0)])  9.53 us
    all_to_all x1, waiting for transfers between devices, per_device(): last = lax.all_to_all(last, 'dp', 0, 0, axis_index_groups=line, tiled=True)  9.43 us
    pallas_call x2, Pallas kernels, image_call(): pl.pallas_call(kernel, out_shape=jax.ShapeDtypeStruct((rows, span), dtype...  8.96 us
    all_to_all x1, starting transfers between devices, per_device(): last = lax.all_to_all(last, 'dp', 0, 0, axis_index_groups=line, tiled=True)  6.92 us
  transfers between devices with their start and end apart: 27, of which 9 were waited for; matrix products, arithmetic and copies ran while one was open for 0% of the time, Pallas kernels for 23%

commit v1 on v0

--- a/solution.py
+++ b/solution.py
@@ -253,7 +253,7 @@
 
 def unit_kernel(
     core, scale, bias, mask, labels, part, there, squares, far, pull, inner, inverses, projected,
-    later_a, later_b, unit, back, weight, factor,
+    later, unit, back, weight, factor,
 ):
     @pl.when(pl.program_id(0) == 0)
     def _():
@@ -287,7 +287,7 @@
                     out[to : to + unit, :] = turned[pl.ds(start, unit), :]
 
 
-def send_kernel(mine, theirs, own, pair, a1, a2, a3, send_b, left, right):
+def send_kernel(mine, theirs, own, pair, later, a1, a2, a3, send_b, left, right):
     slab = mine.shape[0] // (YS * XS)
     many = (XS - 1) * slab
 
@@ -361,25 +361,25 @@
     out[...] = (dot(unit[...], head[...], 1, 1) + there[...].astype(F32)).astype(BF16)
 
 
-def gather_kernel(
-    own_back, near_back, cross_back, far_back, own, near, cross, first, second, high, low
-):
-    far_turned = far_back[...].astype(F32).T.astype(BF16)
+def term_kernel(back, rounded, later, out):
+    out[...] = dot(back[...].astype(F32).T.astype(BF16), rounded[...], 1, 0).astype(BF16)
+
+
+def gather_kernel(own_back, near_back, cross_back, own, near, cross, high, low):
     total = (
         dot(own_back[...], own[...], 1, 0)
         + dot(near_back[...], near[...], 1, 0)
         + dot(cross_back[...], cross[...], 1, 0)
-        + dot(far_turned, first[...], 1, 0)
-        + dot(far_turned, second[...], 1, 0)
     )
     rounded = total.astype(BF16)
     high[...] = rounded
     low[...] = (total - rounded.astype(F32)).astype(BF16)
 
 
-def pull_kernel(high, low, head, texts, inverses, pull, inner, column):
+def pull_kernel(high, low, head, far, texts, inverses, pull, inner, column):
     step = pl.program_id(0)
     total = dot(high[...], head[...], 1, 0) + dot(low[...], head[...], 1, 0)
+    total = total + far[...].astype(F32)
     pull[...] = total
     unit = texts[...].astype(F32) * inverses[:, 1:2]
     dots = jnp.sum(unit * total, axis=1, keepdims=True)
@@ -420,8 +420,6 @@
     count = YS * XS * ZS * CORES
     odd_up = [(i, (i + 1) % count) for i in range(1, count, 2)]
     even_up = [(i, i + 1) for i in range(0, count, 2)]
-    odd_down = [(i, i - 1) for i in range(1, count, 2)]
-    even_down = [(i, (i - 1) % count) for i in range(0, count, 2)]
 
     mine, theirs = call(
         turned_kernel,
@@ -447,14 +445,10 @@
         scratch=[pltpu.VMEM((rows, 128), F32)],
     )
     far_second = lax.ppermute(texts, "dp", even_up)
-    far_image_second = lax.ppermute(images, "dp", odd_down)
     near_text = gate(near_text, own_sent, theirs, mine)
-    near_image = gate(near_image, far_second, far_image_second)
+    near_text = gate(near_text, far_second)
     far_first = lax.ppermute(near_text, "dp", odd_up)
     cross_text = send(near_text, other_core)
-    far_image_first = lax.ppermute(near_image, "dp", even_down)
-    cross_image = send(near_image, other_core)
-
     full = whole((rows, width))
     tile_outs = [
         (square, F32, whole(square)),
@@ -469,10 +463,12 @@
         (projected_b, near_text, own_sent),
     )
     near_there = swap_tensor(near_sent)
+    cross_text = gate(cross_text, near_image)
     cross_part, cross_sent, cross_squares = call(
         tile_kernel, tile_outs, [full, full], (projected_b, cross_text)
     )
     cross_there = swap_tensor(cross_sent)
+    cross_image = send(near_image, other_core)
     far_text, far_part, far_sent, far_squares = call(
         far_kernel,
         [((rows, width), BF16, full)] + tile_outs,
@@ -515,10 +511,10 @@
         scalars
         + [whole((1, rows)), whole(square), whole(tile), whole((8, rows))]
         + [strip(rows, wide), strip(rows, wide), whole((rows, 1)), whole((rows, 2))]
-        + [strip(rows, wide), LATER, LATER],
+        + [strip(rows, wide), LATER],
         known
         + (far_part, far_there, far_squares, far_text, some_pull, inner, inverses, projected)
-        + (far_image_first, cross_image),
+        + (cross_image,),
         grid=(halves,),
         scratch=[pltpu.VMEM(square, BF16), pltpu.VMEM((rows, 1), F32)],
     )
@@ -534,11 +530,18 @@
     a_shape, b_shape = (lines // XS, width // 2), (lines // YS, width // 2)
     sides = (mine, theirs, grad_unit, grad_pair)
     side_specs = [whole((lines, rows))] * 2
+    far_term = call(
+        term_kernel,
+        [((rows, width), BF16, strip(rows, wide))],
+        [whole(square), strip(rows, wide), LATER],
+        (far_back, projected_b, grad_unit),
+        grid=(halves,),
+    )[0]
     send_1, send_2, send_3, send_b = call(
         send_kernel,
         [(a_shape, BF16, a_spec)] * 3 + [(b_shape, BF16, b_spec)],
-        side_specs + [strip(rows, slab)] * 2,
-        sides,
+        side_specs + [strip(rows, slab)] * 2 + [LATER],
+        (*sides, far_term),
         grid=(parts_of,),
         scratch=[pltpu.VMEM((lines // XS * (XS - 1), rows), BF16)] * 2,
     )
@@ -567,24 +570,23 @@
 
     there = image_call(there_kernel, BF16, 1, [LATER], (grad_unit, head, send_b))
 
-    near_back = send(gate(near_back, send_b), lambda i: i - 2)
-    cross_back = send(gate(cross_back, send_b), lambda i: i - 3 if i % 2 else i - 1)
-    far_back = send(gate(far_back, send_b), lambda i: i - 1 if i % 2 else i - 3)
+    far_term = send(gate(far_term, send_b), lambda i: i - 1 if i % 2 else i - 3)
+    near_back = send(gate(near_back, far_term), lambda i: i - 2)
+    cross_back = send(gate(cross_back, far_term), lambda i: i - 3 if i % 2 else i - 1)
     deep = depth // halves
     high, low = call(
         gather_kernel,
         [((rows, depth), BF16, strip(rows, deep))] * 2,
-        [whole(square)] * 4 + [strip(rows, deep)] * 5,
-        (own_back, near_back, cross_back, far_back)
-        + (images, near_image, cross_image, far_image_first, far_image_second),
+        [whole(square)] * 3 + [strip(rows, deep)] * 3,
+        (own_back, near_back, cross_back, images, near_image, cross_image),
         grid=(halves,),
     )
     text_pull, dot_text = call(
         pull_kernel,
         [((rows, width), F32, strip(rows, piece)), ((1, rows), F32, whole((1, rows)))],
         [whole((rows, depth))] * 2
-        + [strip(depth, piece), strip(rows, piece), whole((rows, 2))],
-        (high, low, head, texts, inverses),
+        + [strip(depth, piece), strip(rows, piece), strip(rows, piece), whole((rows, 2))],
+        (high, low, head, far_term, texts, inverses),
         grid=(steps,),
         scratch=[pltpu.VMEM((rows, 1), F32)],
     )

time: 165 us -> 167 us (1.012)
  starting transfers between devices: 66.2 us -> 50.4 us
  waiting for transfers between devices: 41.4 us -> 55.8 us
  local copies, waits for them, and re-layouts: 6.3 us -> 9.43 us
    ppermute x17, waiting for transfers between devices: 22.5 us -> 32.8 us  [send(): return lax.ppermute(block, 'dp', route(target))]
    ppermute x17, starting transfers between devices: 41.6 us -> 33.2 us  [send(): return lax.ppermute(block, 'dp', route(target))]
    ppermute x1, waiting for transfers between devices: 0.01 us -> 7.19 us  [per_device(): far_first = lax.ppermute(near_text, 'dp', odd_up)]
    ppermute x2 -> x0, starting transfers between devices: 4.44 us -> none  [the longest x1 3.16 us: per_device(): far_image_second = lax.ppermute(images, 'dp', odd_down)]
    all_to_all x1, starting transfers between devices: 6.92 us -> 3.49 us  [per_device(): last = lax.all_to_all(last, 'dp', 0, 0, axis_index_groups=line, tiled=True)]
    unnamed x46 -> x52, local copies, waits for them, and re-layouts: 6.3 us -> 9.43 us
    pallas_call x15 -> x16, Pallas kernels: 38.7 us -> 38.9 us  [call(): pl.pallas_call(kernel, out_shape=shapes, grid=grid or (1,), in_specs=ins,...]
  transfers between devices with their start and end apart: 27 -> 25, of which waited for: 9 -> 8; matrix products, arithmetic and copies ran while one was open for 0% -> 0% of each run, Pallas kernels for 23% -> 23%
where the time goes in v1:
time: 167 us; the launch traced here: 166 us
  waiting for transfers between devices  55.8 us (33%)
  starting transfers between devices  50.4 us (30%)
  Pallas kernels  47.9 us (29%)
  local copies, waits for them, and re-layouts  9.43 us (6%)
  between operations  2.35 us (1%)
    pallas_call x16, Pallas kernels, call(): pl.pallas_call(kernel, out_shape=shapes, grid=grid or (1,), in_specs=ins,...  38.9 us
    ppermute x17, starting transfers between devices, send(): return lax.ppermute(block, 'dp', route(target))  33.2 us
    ppermute x17, waiting for transfers between devices, send(): return lax.ppermute(block, 'dp', route(target))  32.8 us
    ppermute x5, starting transfers between devices, swap_tensor(): return lax.ppermute(block, 'tensor', [(0, 1), (1, 0)])  11.2 us
    unnamed x52, local copies, waits for them, and re-layouts  9.43 us
    pallas_call x2, Pallas kernels, image_call(): pl.pallas_call(kernel, out_shape=jax.ShapeDtypeStruct((rows, span), dtype...  8.95 us
    ppermute x5, waiting for transfers between devices, swap_tensor(): return lax.ppermute(block, 'tensor', [(0, 1), (1, 0)])  7.96 us
    all_to_all x1, waiting for transfers between devices, per_device(): last = lax.all_to_all(last, 'dp', 0, 0, axis_index_groups=line, tiled=True)  7.85 us
  transfers between devices with their start and end apart: 25, of which 8 were waited for; matrix products, arithmetic and copies ran while one was open for 0% of the time, Pallas kernels for 23%

profile of v1, /device:TPU:1, one launch (start us, length us, event | category | flops | bytes accessed | tf_op | source)
XLA Modules:
  0.0 166.0 jit_solution(18099013251672094446)
XLA Ops:
  0.6 2.5 %collective-permute-start = (bf16[256,2048]{1,0:T(8,128)(2,1)}, bf16[256,2048]{1,0:T(8,128)(2,1)S(1)}, u32[]{:S(2)}, u32[]{:S(2)}) collective-permute-start(bf16[256,2048]{1,0:T(8,128)(2,1)} %texts.7), channel_id=1, source_target_pairs={{0,4},{2,6},{4,8},{6,10},{8,12},{10,14},{12,16},{14,18},{16,20},{1... | collective-permute-start | bytes 3145736 | tf_op jit(solution)/shard_map/ppermute | solution.py:29
  4.5 7.2 %collective-permute-start.7 = (bf16[256,2048]{1,0:T(8,128)(2,1)}, bf16[256,2048]{1,0:T(8,128)(2,1)S(1)}, u32[]{:S(2)}, u32[]{:S(2)}) collective-permute-start(bf16[256,2048]{1,0:T(8,128)(2,1)} %own.1), channel_id=1, source_target_pairs={{0,252},{2,254},{4,0},{6,2},{8,4},{10,6},{12,8},{14,10},{16,12},{1... | collective-permute-start | bytes 3145736 | tf_op jit(solution)/shard_map/ppermute | solution.py:29
  14.0 1.6 collective-permute-start.1
  16.8 6.5 %shard_map.94 = (f32[256,2048]{1,0:T(8,128)S(1)}, bf16[256,2048]{1,0:T(8,128)(2,1)S(1)}, f32[256,256]{1,0:T(8,128)S(1)}, bf16[272,256]{1,0:T(8,128)(2,1)S(1)}, f32[8,256]{1,0:T(8,128)S(1)}) custom-call(bf16[256,2048]{1,0:T(8,128)(2,1)S(1)} %copy-done.2, bf16[2048,2048]{1,0:T(8,128)(2,1)} %head.7, bf16[256,2048]{1,0:T(8,128)(2,1)S(1)} %copy-done), custom_call_target="tpu_custom_call" | custom-call | tf_op jit(solution)/shard_map/pallas_call | solution.py:86
  23.4 10.1 %collective-permute-done.refs_0_ = bf16[256,2048]{1,0:T(8,128)(2,1)S(1)} collective-permute-done((bf16[256,2048]{1,0:T(8,128)(2,1)}, bf16[256,2048]{1,0:T(8,128)(2,1)S(1)}, u32[]{:S(2)}, u32[]{:S(2)}) %collective-permute-start) | collective-permute-done | bytes 1048608 | tf_op jit(solution)/shard_map/ppermute | solution.py:29
  36.8 2.7 %collective-permute-start.5 = (bf16[2,272,256]{2,1,0:T(8,128)(2,1)S(1)}, bf16[2,272,256]{2,1,0:T(8,128)(2,1)S(1)}, u32[]{:S(2)}, u32[]{:S(2)}) collective-permute-start(bf16[2,272,256]{2,1,0:T(8,128)(2,1)S(1)} %get-tuple-element.53), channel_id=1, source_target_pairs={{0,1},{1,0},{2,3},{3,2},{4,5},{5,4},{6,7},{7,6},{8,9},{9,8},{10,11... | collective-permute-start | bytes 835592 | tf_op jit(solution)/shard_map/ppermute | solution.py:33
  40.6 7.2 %collective-permute-done.3.first = bf16[256,2048]{1,0:T(8,128)(2,1)S(1)} collective-permute-done((bf16[256,2048]{1,0:T(8,128)(2,1)S(1)}, bf16[256,2048]{1,0:T(8,128)(2,1)S(1)}, u32[]{:S(2)}, u32[]{:S(2)}) %collective-permute-start.3) | collective-permute-done | bytes 1048608 | tf_op jit(solution)/shard_map/ppermute | solution.py:450
  48.4 2.7 %collective-permute-start.4 = (bf16[272,256]{1,0:T(8,128)(2,1)S(1)}, bf16[272,256]{1,0:T(8,128)(2,1)S(1)}, u32[]{:S(2)}, u32[]{:S(2)}) collective-permute-start(bf16[272,256]{1,0:T(8,128)(2,1)S(1)} %get-tuple-element.47.later), channel_id=1, source_target_pairs={{0,1},{1,0},{2,3},{3,2},{4,5},{5,4},{6,7},{7,6},{8,9},{9,8},{10,11... | collective-permute-start | bytes 417800 | tf_op jit(solution)/shard_map/ppermute | solution.py:33
  52.4 5.0 %collective-permute-done.5.near_there = bf16[2,272,256]{2,1,0:T(8,128)(2,1)S(1)} collective-permute-done((bf16[2,272,256]{2,1,0:T(8,128)(2,1)S(1)}, bf16[2,272,256]{2,1,0:T(8,128)(2,1)S(1)}, u32[]{:S(2)}, u32[]{:S(2)}) %collective-permute-start.5) | collective-permute-done | bytes 278560 | tf_op jit(solution)/shard_map/ppermute | solution.py:33
  57.4 3.0 %collective-permute-done.8.cross_there = bf16[272,256]{1,0:T(8,128)(2,1)S(1)} collective-permute-done((bf16[272,256]{1,0:T(8,128)(2,1)S(1)}, bf16[272,256]{1,0:T(8,128)(2,1)S(1)}, u32[]{:S(2)}, u32[]{:S(2)}) %collective-permute-start.8) | collective-permute-done | bytes 139296 | tf_op jit(solution)/shard_map/ppermute | solution.py:33
  60.4 3.6 %shard_map.102 = (f32[256,2048]{1,0:T(8,128)}, bf16[256,256]{1,0:T(8,128)(2,1)S(1)}, bf16[256,256]{1,0:T(8,128)(2,1)}, bf16[256,256]{1,0:T(8,128)(2,1)S(1)}, f32[256,1]{1,0:T(8,128)S(1)}, /*index=5*/f32[256,2]{1,0:T(8,128)S(1)}) custom-call(s32[1]{0:T(128)} %bitcast.1.core, f32[1]{0:T(128)S(6)} %copy.30.scale, f32[1]{0:T(128)S(6)} %copy.31.bias, ...), custom_call_target="tpu_custom_call" | custom-call | tf_op jit(solution)/shard_map/pallas_call | solution.py:86
  64.0 2.0 %copy-done.21 = f32[256,2048]{1,0:T(8,128)S(1)} copy-done((f32[256,2048]{1,0:T(8,128)S(1)}, f32[256,2048]{1,0:T(8,128)}, u32[]{:S(2)}) %copy-start.21) | copy-done | bytes 2097176
  66.0 2.5 %shard_map.103 = (bf16[256,2048]{1,0:T(8,128)(2,1)S(1)}, bf16[256,256]{1,0:T(8,128)(2,1)S(1)}) custom-call(s32[1]{0:T(128)} %bitcast.1.core, f32[1]{0:T(128)S(6)} %copy.30.scale, f32[1]{0:T(128)S(6)} %copy.31.bias, s32[1,4]{1,0:T(1,128)S(1)} %copy-done.25, s32[1,256]{1,0:T(1,128)S(1)} %bitcast.7, f32[256,256]{1,0:T(8,128)S(1)} %get-tuple-element.46.part, ...), custom_call_target="tpu_custom_call" | custom-call | tf_op jit(solution)/shard_map/pallas_call | solution.py:86
  68.4 2.4 %collective-permute-start.10 = (bf16[256,2048]{1,0:T(8,128)(2,1)S(1)}, bf16[256,2048]{1,0:T(8,128)(2,1)S(1)}, u32[]{:S(2)}, u32[]{:S(2)}) collective-permute-start(bf16[256,2048]{1,0:T(8,128)(2,1)S(1)} %get-tuple-element.62.later.own.unit), channel_id=1, source_target_pairs={{0,2},{2,0},{4,6},{6,4},{8,10},{10,8},{12,14},{14,12},{16,18},{18,... | collective-permute-start | bytes 3145736 | tf_op jit(solution)/shard_map/ppermute | solution.py:29
  73.1 3.9 %shard_map.105 = (bf16[256,1024]{1,0:T(8,128)(2,1)}, bf16[256,1024]{1,0:T(8,128)(2,1)}, bf16[256,1024]{1,0:T(8,128)(2,1)}, bf16[512,1024]{1,0:T(8,128)(2,1)}) custom-call(bf16[1024,256]{1,0:T(8,128)(2,1)S(1)} %get-tuple-element.45.refs_3_.mine, bf16[1024,256]{1,0:T(8,128)(2,1)S(1)} %collective-permute-done.1.refs_2_.theirs, ...), custom_call_target="tpu_custom_call" | custom-call | tf_op jit(solution)/shard_map/pallas_call | solution.py:86
  79.3 17.3 %collective-permute-done.15.refs_1_.far = bf16[256,2048]{1,0:T(8,128)(2,1)S(1)} collective-permute-done((bf16[256,2048]{1,0:T(8,128)(2,1)S(1)}, bf16[256,2048]{1,0:T(8,128)(2,1)S(1)}, u32[]{:S(2)}, u32[]{:S(2)}) %collective-permute-start.15) | collective-permute-done | bytes 1048608 | tf_op jit(solution)/shard_map/ppermute | solution.py:29
  96.6 4.9 %collective-permute-done.17.cross_back = bf16[256,256]{1,0:T(8,128)(2,1)S(1)} collective-permute-done((bf16[256,256]{1,0:T(8,128)(2,1)S(1)}, bf16[256,256]{1,0:T(8,128)(2,1)S(1)}, u32[]{:S(2)}, u32[]{:S(2)}) %collective-permute-start.17) | collective-permute-done | bytes 131104 | tf_op jit(solution)/shard_map/ppermute | solution.py:29
  101.5 12.0 %collective-permute-start.16 = (bf16[256,256]{1,0:T(8,128)(2,1)}, bf16[256,256]{1,0:T(8,128)(2,1)}, u32[]{:S(2)}, u32[]{:S(2)}) collective-permute-start(bf16[256,256]{1,0:T(8,128)(2,1)} %shard_map.108), channel_id=1, source_target_pairs={{0,252},{2,254},{4,0},{6,2},{8,4},{10,6},{12,8},{14,10},{16,12},{1... | collective-permute-start | bytes 393224 | tf_op jit(solution)/shard_map/ppermute | solution.py:29
  113.5 4.2 %shard_map.106.refs_0_ = bf16[256,1024]{1,0:T(8,128)(2,1)S(1)} custom-call(s32[1]{0:T(128)} %bitcast.half, bf16[256,2048]{1,0:T(8,128)(2,1)S(1)} %get-tuple-element.62.later.own.unit, bf16[2048,2048]{1,0:T(8,128)(2,1)} %head.7, bf16[512,1024]{1,0:T(8,128)(2,1)} %get-tuple-element.64.later.refs_1_), custom_call_target="tpu_custom_call" | custom-call | tf_op jit(solution)/shard_map/pallas_call | solution.py:555
  117.8 2.5 %shard_map.110 = (bf16[256,2048]{1,0:T(8,128)(2,1)S(1)}, bf16[256,2048]{1,0:T(8,128)(2,1)S(1)}) custom-call(bf16[256,256]{1,0:T(8,128)(2,1)S(1)} %get-tuple-element.68.own_back, bf16[256,256]{1,0:T(8,128)(2,1)} %collective-permute-done.16.near_back, bf16[256,256]{1,0:T(8,128)(2,1)S(1)} %collective-permute-done.17.cross_back, ...), custom_call_target="tpu_custom_call" | custom-call | tf_op jit(solution)/shard_map/pallas_call | solution.py:86
  120.3 1.9 %shard_map.112 = (f32[128,1024]{1,0:T(8,128)S(1)}, bf16[128,1024]{1,0:T(8,128)(2,1)S(1)}) custom-call(bf16[1024,256]{1,0:T(8,128)(2,1)S(1)} %copy-done.11, bf16[1024,256]{1,0:T(8,128)(2,1)S(1)} %copy-done.13, bf16[256,2048]{1,0:T(8,128)(2,1)S(1)} %get-tuple-element.62.later.own.unit, bf16[256,2048]{1,0:T(8,128)(2,1)S(1)} %copy-done.7, ...), custom_call_target="tpu_custom_call" | custom-call | tf_op jit(solution)/shard_map/pallas_call | solution.py:86
  122.3 2.1 %shard_map.113 = (f32[128,1024]{1,0:T(8,128)S(1)}, bf16[128,1024]{1,0:T(8,128)(2,1)S(1)}, bf16[128,1024]{1,0:T(8,128)(2,1)S(1)}, bf16[128,1024]{1,0:T(8,128)(2,1)S(1)}) custom-call(bf16[1024,256]{1,0:T(8,128)(2,1)S(1)} %copy-done.11, bf16[1024,256]{1,0:T(8,128)(2,1)S(1)} %copy-done.13, bf16[256,2048]{1,0:T(8,128)(2,1)S(1)} %get-tuple-element.62.later.own.unit, ...), custom_call_target="tpu_custom_call" | custom-call | tf_op jit(solution)/shard_map/pallas_call | solution.py:86
  124.4 1.8 %collective-permute-start.18 = (bf16[256,1024]{1,0:T(8,128)(2,1)S(1)}, bf16[256,1024]{1,0:T(8,128)(2,1)S(1)}, u32[]{:S(2)}, u32[]{:S(2)}) collective-permute-start(bf16[256,1024]{1,0:T(8,128)(2,1)S(1)} %shard_map.114), channel_id=1, source_target_pairs={{0,1},{1,0},{2,3},{3,2},{4,5},{5,4},{6,7},{7,6},{8,9},{9,8},{10,11... | collective-permute-start | bytes 1572872 | tf_op jit(solution)/shard_map/ppermute | solution.py:33
  127.7 2.3 %collective-permute-start.20 = (bf16[128,1024]{1,0:T(8,128)(2,1)S(1)}, bf16[128,1024]{1,0:T(8,128)(2,1)S(1)}, u32[]{:S(2)}, u32[]{:S(2)}) collective-permute-start(bf16[128,1024]{1,0:T(8,128)(2,1)S(1)} %get-tuple-element.72.later), channel_id=1, source_target_pairs={{0,128},{2,130},{4,132},{6,134},{8,136},{10,138},{12,140},{14,142}... | collective-permute-start | bytes 786440 | tf_op jit(solution)/shard_map/ppermute | solution.py:29
  130.0 8.5 %shard_map.116 = (f32[256,2048]{1,0:T(8,128)}, f32[1,256]{1,0:T(1,128)S(1)}) custom-call(bf16[256,2048]{1,0:T(8,128)(2,1)S(1)} %get-tuple-element.71.refs_1_.high, bf16[256,2048]{1,0:T(8,128)(2,1)S(1)} %get-tuple-element.74.low, bf16[2048,2048]{1,0:T(8,128)(2,1)} %head.7, bf16[256,2048]{1,0:T(8,128)(2,1)S(1)} %collective-permute-done.15.refs_1_.far, ...), custom_call_target="tpu_custom_call" | custom-call | tf_op jit(solution)/shard_map/pallas_call | solution.py:86
  138.5 3.5 %collective-permute-start.19 = (f32[1,256]{1,0:T(1,128)S(1)}, f32[1,256]{1,0:T(1,128)S(1)}, u32[]{:S(2)}, u32[]{:S(2)}) collective-permute-start(f32[1,256]{1,0:T(1,128)S(1)} %get-tuple-element.76.inner), channel_id=1, source_target_pairs={{0,1},{1,0},{2,3},{3,2},{4,5},{5,4},{6,7},{7,6},{8,9},{9,8},{10,11... | collective-permute-start | bytes 3080 | tf_op jit(solution)/shard_map/ppermute | solution.py:33
  142.0 1.6 copy-done.8
  145.3 3.5 %all-to-all-start = ((bf16[8,16,2048]{2,1,0:T(8,128)(2,1)}), bf16[8,16,2048]{2,1,0:T(8,128)(2,1)S(1)}, u32[]{:S(2)}, u32[]{:S(2)}) async-start(bf16[8,16,2048]{2,1,0:T(8,128)(2,1)} %bitcast.5), calls=%async_computation | async-start | bytes 1048576 | tf_op jit(solution)/shard_map/all_to_all | solution.py:629
  148.8 1.6 copy-done.9
  150.4 2.2 %shard_map.117 = bf16[256,2048]{1,0:T(8,128)(2,1)} custom-call(f32[256,2048]{1,0:T(8,128)S(1)} %copy-done.9, bf16[256,2048]{1,0:T(8,128)(2,1)S(1)} %copy-done.1, f32[256,2]{1,0:T(8,128)S(1)} %get-tuple-element.60.inverses, f32[1,256]{1,0:T(1,128)S(1)} %get-tuple-element.76.inner, f32[1,256]{1,0:T(1,128)S(1)} %collective-permute-done.19.there.refs_2_), custom_call_target="tpu_custom_call" | custom-call | tf_op jit(solution)/shard_map/pallas_call | solution.py:86
  152.6 4.8 %shard_map.115 = bf16[256,1024]{1,0:T(8,128)(2,1)} custom-call(s32[1]{0:T(128)} %bitcast.half, bf16[256,2048]{1,0:T(8,128)(2,1)S(1)} %get-tuple-element.62.later.own.unit, bf16[2048,2048]{1,0:T(8,128)(2,1)} %head.7, bf16[256,1024]{1,0:T(8,128)(2,1)S(1)} %copy-done.23), custom_call_target="tpu_custom_call" | custom-call | tf_op jit(solution)/shard_map/pallas_call | solution.py:555
  157.4 7.9 %all-to-all-done.blocks = bf16[8,16,2048]{2,1,0:T(8,128)(2,1)S(1)} async-done(((bf16[8,16,2048]{2,1,0:T(8,128)(2,1)}), bf16[8,16,2048]{2,1,0:T(8,128)(2,1)S(1)}, u32[]{:S(2)}, u32[]{:S(2)}) %all-to-all-start) | async-done | bytes 524320 | tf_op jit(solution)/shard_map/all_to_all | solution.py:629
  (99 shorter events, 18.4 us)
Async XLA Ops:
  0.6 32.8 %collective-permute-start = (bf16[256,2048]{1,0:T(8,128)(2,1)}, bf16[256,2048]{1,0:T(8,128)(2,1)S(1)}, u32[]{:S(2)}, u32[]{:S(2)}) collective-permute-start(bf16[256,2048]{1,0:T(8,128)(2,1)} %texts.7), channel_id=1, source_target_pairs={{0,4},{2,6},{4,8},{6,10},{8,12},{10,14},{12,16},{14,18},{16,20},{1... | collective-permute-start | bytes 3145736 | tf_op jit(solution)/shard_map/ppermute | solution.py:29
  3.2 30.2 %collective-permute-start.2 = (bf16[256,2048]{1,0:T(8,128)(2,1)}, bf16[256,2048]{1,0:T(8,128)(2,1)S(1)}, u32[]{:S(2)}, u32[]{:S(2)}) collective-permute-start(bf16[256,2048]{1,0:T(8,128)(2,1)} %texts.7), channel_id=1, source_target_pairs={{0,2},{4,6},{8,10},{12,14},{16,18},{20,22},{24,26},{28,30},{32,34}... | collective-permute-start | bytes 3145736 | tf_op jit(solution)/shard_map/ppermute | solution.py:447
  4.5 31.6 %collective-permute-start.7 = (bf16[256,2048]{1,0:T(8,128)(2,1)}, bf16[256,2048]{1,0:T(8,128)(2,1)S(1)}, u32[]{:S(2)}, u32[]{:S(2)}) collective-permute-start(bf16[256,2048]{1,0:T(8,128)(2,1)} %own.1), channel_id=1, source_target_pairs={{0,252},{2,254},{4,0},{6,2},{8,4},{10,6},{12,8},{14,10},{16,12},{1... | collective-permute-start | bytes 3145736 | tf_op jit(solution)/shard_map/ppermute | solution.py:29
  14.0 59.1 %copy-start.10 = (bf16[1024,256]{1,0:T(8,128)(2,1)}, bf16[1024,256]{1,0:T(8,128)(2,1)S(1)}, u32[]{:S(2)}) copy-start(bf16[1024,256]{1,0:T(8,128)(2,1)S(1)} %get-tuple-element.45.refs_3_.mine) | copy-start | bytes 1572868
  14.0 9.3 %collective-permute-start.1 = (bf16[1024,256]{1,0:T(8,128)(2,1)S(1)}, bf16[1024,256]{1,0:T(8,128)(2,1)S(1)}, u32[]{:S(2)}, u32[]{:S(2)}) collective-permute-start(bf16[1024,256]{1,0:T(8,128)(2,1)S(1)} %get-tuple-element.44), channel_id=1, source_target_pairs={{0,2},{2,0},{4,6},{6,4},{8,10},{10,8},{12,14},{14,12},{16,18},{18,... | collective-permute-start | bytes 1572872 | tf_op jit(solution)/shard_map/ppermute | solution.py:29
  23.3 10.1 %copy-start.20 = (f32[256,2048]{1,0:T(8,128)}, f32[256,2048]{1,0:T(8,128)S(1)}, u32[]{:S(2)}) copy-start(f32[256,2048]{1,0:T(8,128)S(1)} %get-tuple-element.61.projected) | copy-start | bytes 6291460
  23.4 49.7 %copy-start.12 = (bf16[1024,256]{1,0:T(8,128)(2,1)}, bf16[1024,256]{1,0:T(8,128)(2,1)S(1)}, u32[]{:S(2)}) copy-start(bf16[1024,256]{1,0:T(8,128)(2,1)S(1)} %collective-permute-done.1.refs_2_.theirs) | copy-start | bytes 1572868
  33.4 6.1 %collective-permute-start.6 = (bf16[256,2048]{1,0:T(8,128)(2,1)S(1)}, bf16[256,2048]{1,0:T(8,128)(2,1)S(1)}, u32[]{:S(2)}, u32[]{:S(2)}) collective-permute-start(bf16[256,2048]{1,0:T(8,128)(2,1)S(1)} %shard_map.97.text.near), channel_id=1, source_target_pairs={{0,2},{2,0},{4,6},{6,4},{8,10},{10,8},{12,14},{14,12},{16,18},{18,... | collective-permute-start | bytes 3145736 | tf_op jit(solution)/shard_map/ppermute | solution.py:29
  34.7 13.0 %collective-permute-start.3 = (bf16[256,2048]{1,0:T(8,128)(2,1)S(1)}, bf16[256,2048]{1,0:T(8,128)(2,1)S(1)}, u32[]{:S(2)}, u32[]{:S(2)}) collective-permute-start(bf16[256,2048]{1,0:T(8,128)(2,1)S(1)} %shard_map.97.text.near), channel_id=1, source_target_pairs={{2,4},{6,8},{10,12},{14,16},{18,20},{22,24},{26,28},{30,32},{34,36... | collective-permute-start | bytes 3145736 | tf_op jit(solution)/shard_map/ppermute | solution.py:450
  36.1 27.9 %collective-permute-start.9 = (bf16[256,2048]{1,0:T(8,128)(2,1)S(1)}, bf16[256,2048]{1,0:T(8,128)(2,1)S(1)}, u32[]{:S(2)}, u32[]{:S(2)}) collective-permute-start(bf16[256,2048]{1,0:T(8,128)(2,1)S(1)} %collective-permute-done.7.refs_1_.near), channel_id=1, source_target_pairs={{0,2},{2,0},{4,6},{6,4},{8,10},{10,8},{12,14},{14,12},{16,18},{18,... | collective-permute-start | bytes 3145736 | tf_op jit(solution)/shard_map/ppermute | solution.py:29
  36.8 11.0 %copy-start.17 = (bf16[256,2048]{1,0:T(8,128)(2,1)S(1)}, bf16[256,2048]{1,0:T(8,128)(2,1)}, u32[]{:S(2)}) copy-start(bf16[256,2048]{1,0:T(8,128)(2,1)} %copy-done.16) | copy-start | bytes 3145732
  36.8 20.6 %collective-permute-start.5 = (bf16[2,272,256]{2,1,0:T(8,128)(2,1)S(1)}, bf16[2,272,256]{2,1,0:T(8,128)(2,1)S(1)}, u32[]{:S(2)}, u32[]{:S(2)}) collective-permute-start(bf16[2,272,256]{2,1,0:T(8,128)(2,1)S(1)} %get-tuple-element.53), channel_id=1, source_target_pairs={{0,1},{1,0},{2,3},{3,2},{4,5},{5,4},{6,7},{7,6},{8,9},{9,8},{10,11... | collective-permute-start | bytes 835592 | tf_op jit(solution)/shard_map/ppermute | solution.py:33
  40.1 20.3 %copy-start.1 = (bf16[256,2048]{1,0:T(8,128)(2,1)S(1)}, bf16[256,2048]{1,0:T(8,128)(2,1)}, u32[]{:S(2)}) copy-start(bf16[256,2048]{1,0:T(8,128)(2,1)} %texts.7) | copy-start | bytes 3145732
  40.1 20.3 %copy-start.24 = (s32[256]{0:T(256)S(1)}, s32[256]{0:T(256)}, u32[]{:S(2)}) copy-start(s32[256]{0:T(256)} %param.11) | copy-start | bytes 3076
  40.1 20.2 %copy-start.25 = (s32[1,4]{1,0:T(1,128)S(1)}, s32[1,4]{1,0:T(1,128)}, u32[]{:S(2)}) copy-start(s32[1,4]{1,0:T(1,128)} %mask.3) | copy-start | bytes 52
  40.1 20.2 %collective-permute-start.8 = (bf16[272,256]{1,0:T(8,128)(2,1)S(1)}, bf16[272,256]{1,0:T(8,128)(2,1)S(1)}, u32[]{:S(2)}, u32[]{:S(2)}) collective-permute-start(bf16[272,256]{1,0:T(8,128)(2,1)S(1)} %get-tuple-element.56), channel_id=1, source_target_pairs={{0,1},{1,0},{2,3},{3,2},{4,5},{5,4},{6,7},{7,6},{8,9},{9,8},{10,11... | collective-permute-start | bytes 417800 | tf_op jit(solution)/shard_map/ppermute | solution.py:33
  48.4 15.6 %collective-permute-start.4 = (bf16[272,256]{1,0:T(8,128)(2,1)S(1)}, bf16[272,256]{1,0:T(8,128)(2,1)S(1)}, u32[]{:S(2)}, u32[]{:S(2)}) collective-permute-start(bf16[272,256]{1,0:T(8,128)(2,1)S(1)} %get-tuple-element.47.later), channel_id=1, source_target_pairs={{0,1},{1,0},{2,3},{3,2},{4,5},{5,4},{6,7},{7,6},{8,9},{9,8},{10,11... | collective-permute-start | bytes 417800 | tf_op jit(solution)/shard_map/ppermute | solution.py:33
  68.4 4.7 %collective-permute-start.10 = (bf16[256,2048]{1,0:T(8,128)(2,1)S(1)}, bf16[256,2048]{1,0:T(8,128)(2,1)S(1)}, u32[]{:S(2)}, u32[]{:S(2)}) collective-permute-start(bf16[256,2048]{1,0:T(8,128)(2,1)S(1)} %get-tuple-element.62.later.own.unit), channel_id=1, source_target_pairs={{0,2},{2,0},{4,6},{6,4},{8,10},{10,8},{12,14},{14,12},{16,18},{18,... | collective-permute-start | bytes 3145736 | tf_op jit(solution)/shard_map/ppermute | solution.py:29
  77.0 19.6 %collective-permute-start.15 = (bf16[256,2048]{1,0:T(8,128)(2,1)S(1)}, bf16[256,2048]{1,0:T(8,128)(2,1)S(1)}, u32[]{:S(2)}, u32[]{:S(2)}) collective-permute-start(bf16[256,2048]{1,0:T(8,128)(2,1)S(1)} %shard_map.107), channel_id=1, source_target_pairs={{0,250},{2,0},{4,254},{6,4},{8,2},{10,8},{12,6},{14,12},{16,10},{1... | collective-permute-start | bytes 3145736 | tf_op jit(solution)/shard_map/ppermute | solution.py:29
  77.6 44.6 %collective-permute-start.11 = (bf16[512,1024]{1,0:T(8,128)(2,1)}, bf16[512,1024]{1,0:T(8,128)(2,1)}, u32[]{:S(2)}, u32[]{:S(2)}) collective-permute-start(bf16[512,1024]{1,0:T(8,128)(2,1)} %get-tuple-element.64.later.refs_1_), channel_id=1, source_target_pairs={{0,128},{2,130},{4,132},{6,134},{8,136},{10,138},{12,140},{14,142}... | collective-permute-start | bytes 3145736 | tf_op jit(solution)/shard_map/ppermute | solution.py:29
  77.8 42.4 %collective-permute-start.14 = (bf16[256,1024]{1,0:T(8,128)(2,1)}, bf16[256,1024]{1,0:T(8,128)(2,1)}, u32[]{:S(2)}, u32[]{:S(2)}) collective-permute-start(bf16[256,1024]{1,0:T(8,128)(2,1)} %get-tuple-element.67), channel_id=1, source_target_pairs={{0,96},{2,98},{4,100},{6,102},{8,104},{10,106},{12,108},{14,110},{... | collective-permute-start | bytes 1572872 | tf_op jit(solution)/shard_map/ppermute | solution.py:29
  77.8 42.4 %collective-permute-start.12 = (bf16[256,1024]{1,0:T(8,128)(2,1)}, bf16[256,1024]{1,0:T(8,128)(2,1)}, u32[]{:S(2)}, u32[]{:S(2)}) collective-permute-start(bf16[256,1024]{1,0:T(8,128)(2,1)} %get-tuple-element.65), channel_id=1, source_target_pairs={{0,64},{2,66},{4,68},{6,70},{8,72},{10,74},{12,76},{14,78},{16,80}... | collective-permute-start | bytes 1572872 | tf_op jit(solution)/shard_map/ppermute | solution.py:29
  77.8 42.4 %collective-permute-start.13 = (bf16[256,1024]{1,0:T(8,128)(2,1)}, bf16[256,1024]{1,0:T(8,128)(2,1)}, u32[]{:S(2)}, u32[]{:S(2)}) collective-permute-start(bf16[256,1024]{1,0:T(8,128)(2,1)} %get-tuple-element.66), channel_id=1, source_target_pairs={{0,32},{2,34},{4,36},{6,38},{8,40},{10,42},{12,44},{14,46},{16,48}... | collective-permute-start | bytes 1572872 | tf_op jit(solution)/shard_map/ppermute | solution.py:29
  96.6 4.9 %collective-permute-start.17 = (bf16[256,256]{1,0:T(8,128)(2,1)S(1)}, bf16[256,256]{1,0:T(8,128)(2,1)S(1)}, u32[]{:S(2)}, u32[]{:S(2)}) collective-permute-start(bf16[256,256]{1,0:T(8,128)(2,1)S(1)} %shard_map.109), channel_id=1, source_target_pairs={{0,254},{2,252},{4,2},{6,0},{8,6},{10,4},{12,10},{14,8},{16,14},{1... | collective-permute-start | bytes 393224 | tf_op jit(solution)/shard_map/ppermute | solution.py:29
  101.5 16.2 %collective-permute-start.16 = (bf16[256,256]{1,0:T(8,128)(2,1)}, bf16[256,256]{1,0:T(8,128)(2,1)}, u32[]{:S(2)}, u32[]{:S(2)}) collective-permute-start(bf16[256,256]{1,0:T(8,128)(2,1)} %shard_map.108), channel_id=1, source_target_pairs={{0,252},{2,254},{4,0},{6,2},{8,4},{10,6},{12,8},{14,10},{16,12},{1... | collective-permute-start | bytes 393224 | tf_op jit(solution)/shard_map/ppermute | solution.py:29
  124.4 20.2 %collective-permute-start.18 = (bf16[256,1024]{1,0:T(8,128)(2,1)S(1)}, bf16[256,1024]{1,0:T(8,128)(2,1)S(1)}, u32[]{:S(2)}, u32[]{:S(2)}) collective-permute-start(bf16[256,1024]{1,0:T(8,128)(2,1)S(1)} %shard_map.114), channel_id=1, source_target_pairs={{0,1},{1,0},{2,3},{3,2},{4,5},{5,4},{6,7},{7,6},{8,9},{9,8},{10,11... | collective-permute-start | bytes 1572872 | tf_op jit(solution)/shard_map/ppermute | solution.py:33
  126.2 12.3 %collective-permute-start.23 = (bf16[128,1024]{1,0:T(8,128)(2,1)S(1)}, bf16[128,1024]{1,0:T(8,128)(2,1)S(1)}, u32[]{:S(2)}, u32[]{:S(2)}) collective-permute-start(bf16[128,1024]{1,0:T(8,128)(2,1)S(1)} %get-tuple-element.80), channel_id=1, source_target_pairs={{0,96},{2,98},{4,100},{6,102},{8,104},{10,106},{12,108},{14,110},{... | collective-permute-start | bytes 786440 | tf_op jit(solution)/shard_map/ppermute | solution.py:29
  126.2 17.3 %collective-permute-start.21 = (bf16[128,1024]{1,0:T(8,128)(2,1)S(1)}, bf16[128,1024]{1,0:T(8,128)(2,1)S(1)}, u32[]{:S(2)}, u32[]{:S(2)}) collective-permute-start(bf16[128,1024]{1,0:T(8,128)(2,1)S(1)} %get-tuple-element.78), channel_id=1, source_target_pairs={{0,64},{2,66},{4,68},{6,70},{8,72},{10,74},{12,76},{14,78},{16,80}... | collective-permute-start | bytes 786440 | tf_op jit(solution)/shard_map/ppermute | solution.py:29
  126.2 17.3 %collective-permute-start.22 = (bf16[128,1024]{1,0:T(8,128)(2,1)S(1)}, bf16[128,1024]{1,0:T(8,128)(2,1)S(1)}, u32[]{:S(2)}, u32[]{:S(2)}) collective-permute-start(bf16[128,1024]{1,0:T(8,128)(2,1)S(1)} %get-tuple-element.79), channel_id=1, source_target_pairs={{0,32},{2,34},{4,36},{6,38},{8,40},{10,42},{12,44},{14,46},{16,48}... | collective-permute-start | bytes 786440 | tf_op jit(solution)/shard_map/ppermute | solution.py:29
  127.7 15.9 %collective-permute-start.20 = (bf16[128,1024]{1,0:T(8,128)(2,1)S(1)}, bf16[128,1024]{1,0:T(8,128)(2,1)S(1)}, u32[]{:S(2)}, u32[]{:S(2)}) collective-permute-start(bf16[128,1024]{1,0:T(8,128)(2,1)S(1)} %get-tuple-element.72.later), channel_id=1, source_target_pairs={{0,128},{2,130},{4,132},{6,134},{8,136},{10,138},{12,140},{14,142}... | collective-permute-start | bytes 786440 | tf_op jit(solution)/shard_map/ppermute | solution.py:29
  138.5 6.0 %collective-permute-start.19 = (f32[1,256]{1,0:T(1,128)S(1)}, f32[1,256]{1,0:T(1,128)S(1)}, u32[]{:S(2)}, u32[]{:S(2)}) collective-permute-start(f32[1,256]{1,0:T(1,128)S(1)} %get-tuple-element.76.inner), channel_id=1, source_target_pairs={{0,1},{1,0},{2,3},{3,2},{4,5},{5,4},{6,7},{7,6},{8,9},{9,8},{10,11... | collective-permute-start | bytes 3080 | tf_op jit(solution)/shard_map/ppermute | solution.py:33
  145.3 19.9 %all-to-all-start = ((bf16[8,16,2048]{2,1,0:T(8,128)(2,1)}), bf16[8,16,2048]{2,1,0:T(8,128)(2,1)S(1)}, u32[]{:S(2)}, u32[]{:S(2)}) async-start(bf16[8,16,2048]{2,1,0:T(8,128)(2,1)} %bitcast.5), calls=%async_computation | async-start | bytes 1048576 | tf_op jit(solution)/shard_map/all_to_all | solution.py:629
  (19 other events, 50.9 us)
